TPU v7x, 256 devices: a whole 4x4x8 slice. The times are simulated.
256 devices in a mesh: clip: 8 (over y_hi, x), seq: 32 (over z, y_lo, core).
Axes of the slice: x: 4, y: 4 (y_hi: 2, y_lo: 2; y = y_hi * 2 + y_lo), z: 8, core: 2. Of those that a mesh axis runs over, the one named last changes fastest.
Arguments:
- latent: float32 [8, 64, 8192], P('clip', None, 'seq'), may hold values from -6 to 6
- sample_noise: float32 [8, 64, 8192], P('clip', None, 'seq'), may hold values from -6 to 6
- vel_cond: bfloat16 [8, 64, 8192], P('clip', None, 'seq'), may hold values from -6 to 6
- vel_uncond: bfloat16 [8, 64, 8192], P('clip', None, 'seq'), may hold values from -6 to 6
- step_index: int32 [1], replicated, may hold values from 0 to 15
- embed_w: bfloat16 [64, 3072], replicated, may hold values from -0.75 to 0.75
- gate_scale: float32 [8, 3072], P('clip'), may hold values from 0.5 to 1.5
- attn_vals: bfloat16 [8, 8192, 1536], P('clip', 'seq'), may hold values from -6 to 6
- out_w: bfloat16 [1536, 3072], P(None, 'clip'), may hold values from -0.15625 to 0.15625
- cotangent: bfloat16 [8, 8192, 3072], P('clip', 'seq'), may hold values from -6 to 6
- rewards: float32 [8], P('clip'), may hold values from 0 to 2
Outputs:
- block_out: bfloat16 [8, 8192, 3072], P('clip', 'seq')
- grad_attn: bfloat16 [8, 8192, 1536], P('clip', 'seq')
- grad_out_w: float32 [1536, 3072], P('seq', 'clip')
- grad_embed_w: float32 [8, 64, 3072], P('clip')
Inputs may be any that keep to these rules, and one draw needn't show every extreme that they name: `step_index`: index of the step among the 16 steps of the roster.
All inputs are finite; a program needn't handle non-finite values.
Results may differ from a plain program's by a relative error of at most 0.017.
Values may be sent and summed in bfloat16 or wider, within the bound.
A program may use at most 128 MiB of HBM per device.

v0:
```python
import jax
import jax.numpy as jnp
from jax import lax
from jax.sharding import PartitionSpec as P

NSTEPS = 16


SHIFT_FACTOR = 7.0
GUIDANCE = 6.0
NOISE_LEVEL = 0.3


def sigma_level(index):
    tval = 1.0 - index.astype(jnp.float32) / NSTEPS
    return SHIFT_FACTOR * tval / (1.0 + (SHIFT_FACTOR - 1.0) * tval)


def local(
    latent,
    sample_noise,
    vel_cond,
    vel_uncond,
    step_index,
    embed_w,
    gate_scale,
    attn_vals,
    out_w,
    cotangent,
    rewards,
):
    reward_sum = lax.psum(rewards, "clip")
    advantage = rewards[0] - reward_sum[0] / lax.axis_size("clip")
    sig_now = sigma_level(step_index[0])
    sig_next = sigma_level(step_index[0] + 1)
    uncond = vel_uncond[0].astype(jnp.float32)
    guided = uncond + GUIDANCE * (vel_cond[0].astype(jnp.float32) - uncond)
    spread = NOISE_LEVEL * jnp.sqrt(sig_now - sig_next)
    sampled = (latent[0] + (sig_next - sig_now) * guided + spread * sample_noise[0]).astype(
        jnp.bfloat16
    )
    embedded = jnp.einsum("cl,cd->ld", sampled, embed_w, preferred_element_type=jnp.float32)
    scaled = (cotangent[0].astype(jnp.float32) * advantage).astype(jnp.bfloat16)
    branch = (scaled.astype(jnp.float32) * gate_scale[0]).astype(jnp.bfloat16)
    values = attn_vals[0]
    contract_last = (((1,), (1,)), ((), ()))
    contract_first = (((0,), (0,)), ((), ()))
    full_weight = lax.all_gather(out_w, "clip", axis=1, tiled=True)
    projected = jnp.dot(values, full_weight, preferred_element_type=jnp.float32)
    grad_values = lax.dot_general(
        branch, full_weight, contract_last, preferred_element_type=jnp.float32
    )
    weight_term = lax.dot_general(
        values, branch, contract_first, preferred_element_type=jnp.float32
    )
    block_out = (embedded + gate_scale[0] * projected).astype(jnp.bfloat16)
    row_sums = lax.psum_scatter(weight_term, "seq", scatter_dimension=0, tiled=True)
    grad_w = lax.psum_scatter(row_sums, "clip", scatter_dimension=1, tiled=True)
    embed_term = jnp.einsum("cl,ld->cd", sampled, scaled, preferred_element_type=jnp.float32)
    grad_embed = lax.psum(embed_term, "seq")
    return (block_out[None], grad_values.astype(jnp.bfloat16)[None], grad_w, grad_embed[None])


def solution(mesh):
    in_specs = (
        P("clip", None, "seq"),
        P("clip", None, "seq"),
        P("clip", None, "seq"),
        P("clip", None, "seq"),
        P(),
        P(),
        P("clip", None),
        P("clip", "seq", None),
        P(None, "clip"),
        P("clip", "seq", None),
        P("clip"),
    )
    out_specs = (
        P("clip", "seq", None),
        P("clip", "seq", None),
        P("seq", "clip"),
        P("clip", None, None),
    )
    return jax.shard_map(local, mesh=mesh, in_specs=in_specs, out_specs=out_specs, check_vma=False)
```

profile of v0, /device:TPU:1, one launch (start us, length us, event | category | flops | bytes accessed | tf_op | source)
XLA Modules:
  0.0 579.5 jit_solution(1873939354662667426)
XLA Ops:
  8.0 0.0 copy-start
  8.0 0.0 reduce-scatter.7.cloned.1.call-start
  8.8 22.1 %psum.14 = f32[1]{0:T(128)} all-reduce(f32[1]{0:T(128)} %param.21), channel_id=1, replica_groups=mesh['clip'=8,'seq'=32] {'clip'}, use_global_device_ids=true, to_apply=%region_0.0 | all-reduce | flops 1 | bytes 8 | tf_op jit(solution)/shard_map/psum | solution.py:32
  31.5 9.4 %convolution_bitcast_fusion = f32[1536,3072]{0,1:T(8,128)} fusion(f32[3072]{0:T(1024)} %bitcast.76, bf16[1,256,3072]{2,1,0:T(8,128)(2,1)} %param.20, f32[]{:T(128)} %bitcast.9, bf16[1,256,1536]{2,1,0:T(8,128)(2,1)S(1)} %copy-done), kind=kOutput, calls=%fused_computation | convolution fusion | flops 2420637696 | bytes 21245956 | tf_op jit(solution)/shard_map/dot_general | solution.py:53
  40.9 18.7 %copy.17 = f32[1536,3072]{1,0:T(8,128)} copy(f32[1536,3072]{0,1:T(8,128)} %convolution_bitcast_fusion) | data formatting | bytes 37748736
  59.6 0.0 reduce-scatter.7.cloned.1.call-update
  59.6 0.0 copy-start.3
  59.6 0.0 all-gather.2.cloned.1.call-start
  59.7 0.5 all-gather.2.cloned.1.call-update
  60.2 0.0 reduce-scatter.5.cloned.1.call-start
  60.3 276.5 %reduce-scatter.7.cloned.1.call-done = f32[48,3072]{1,0:T(8,128)} async-done(((f32[1536,3072]{1,0:T(8,128)}), f32[48,3072]{1,0:T(8,128)}) %reduce-scatter.7.cloned.1.call-update) | async-done | bytes 589840
  336.8 2.7 copy.18
  339.5 0.0 reduce-scatter.5.cloned.1.call-update
  339.5 0.0 all-reduce.2.cloned.1.call-start
  340.4 1.4 convolution_bitcast_fusion.1
  341.7 0.0 all-reduce.2.cloned.1.call-update
  341.8 0.0 all-gather.2.cloned.1.call-done
  341.8 5.3 convolution_multiply_fusion
  347.2 1.8 fusion.1
  348.9 3.7 fusion.2
  352.6 64.7 %reduce-scatter.5.cloned.1.call-done = f32[48,384]{0,1:T(8,128)} async-done(((f32[48,3072]{0,1:T(8,128)}), f32[48,384]{0,1:T(8,128)}) %reduce-scatter.5.cloned.1.call-update) | async-done | bytes 73744 | tf_op jit(solution)/shard_map/reduce_scatter | solution.py:58
  417.3 1.7 copy.16
  419.0 151.0 %all-reduce.2.cloned.1.call-done = f32[1,64,3072]{2,1,0:T(8,128)} async-done(((f32[1,64,3072]{2,1,0:T(8,128)}), f32[1,64,3072]{2,1,0:T(8,128)}) %all-reduce.2.cloned.1.call-update) | async-done | bytes 786448 | tf_op jit(solution)/shard_map/psum | solution.py:60
  570.0 2.1 copy.22
  (16 shorter events, 0.0 us)
Async XLA Ops:
  8.0 23.5 %copy-start = (bf16[1,256,1536]{2,1,0:T(8,128)(2,1)S(1)}, bf16[1,256,1536]{2,1,0:T(8,128)(2,1)}, u32[]{:S(2)}) copy-start(bf16[1,256,1536]{2,1,0:T(8,128)(2,1)} %param.18) | copy-start | bytes 2359300
  8.0 328.8 %reduce-scatter.7.cloned.1.call-start = ((), (), s32[]{:S(2)}) async-start(), calls=%async_computation.5 | async-start | bytes 19464192
  59.6 280.7 %copy-start.1 = (bf16[1,256,3072]{2,1,0:T(8,128)(2,1)S(1)}, bf16[1,256,3072]{2,1,0:T(8,128)(2,1)}, u32[]{:S(2)}) copy-start(bf16[1,256,3072]{2,1,0:T(8,128)(2,1)} %param.20) | copy-start | bytes 4718596
  59.6 280.7 %copy-start.3 = (f32[1,64,256]{2,1,0:T(8,128)S(1)}, f32[1,64,256]{2,1,0:T(8,128)}, u32[]{:S(2)}) copy-start(f32[1,64,256]{2,1,0:T(8,128)} %param.11) | copy-start | bytes 196612
  59.6 280.7 %copy-start.4 = (f32[1,64,256]{2,1,0:T(8,128)S(1)}, f32[1,64,256]{2,1,0:T(8,128)}, u32[]{:S(2)}) copy-start(f32[1,64,256]{2,1,0:T(8,128)} %param.12) | copy-start | bytes 196612
  59.6 280.7 %copy-start.5 = (bf16[1,64,256]{2,1,0:T(8,128)(2,1)S(1)}, bf16[1,64,256]{2,1,0:T(8,128)(2,1)}, u32[]{:S(2)}) copy-start(bf16[1,64,256]{2,1,0:T(8,128)(2,1)} %param.13) | copy-start | bytes 98308
  59.6 280.7 %copy-start.6 = (bf16[1,64,256]{2,1,0:T(8,128)(2,1)S(1)}, bf16[1,64,256]{2,1,0:T(8,128)(2,1)}, u32[]{:S(2)}) copy-start(bf16[1,64,256]{2,1,0:T(8,128)(2,1)} %param.14) | copy-start | bytes 98308
  59.6 282.1 %all-gather.2.cloned.1.call-start = ((), (), s32[]{:S(2)}) async-start(), calls=%async_computation.2 | async-start | bytes 10616832 | tf_op jit(solution)/shard_map/all_gather | solution.py:48
  60.2 281.6 %copy-start.7 = (f32[1,3072]{1,0:T(1,128)S(1)}, f32[1,3072]{1,0:T(1,128)}, u32[]{:S(2)}) copy-start(f32[1,3072]{1,0:T(1,128)} %param.17) | copy-start | bytes 36868
  60.2 357.1 %reduce-scatter.5.cloned.1.call-start = ((), (), s32[]{:S(2)}) async-start(), calls=%async_computation.3 | async-start | bytes 1769472 | tf_op jit(solution)/shard_map/reduce_scatter | solution.py:58
  339.5 230.5 %all-reduce.2.cloned.1.call-start = ((), (), s32[]{:S(2)}) async-start(), calls=%async_computation.4 | async-start | bytes 1572864 | tf_op jit(solution)/shard_map/psum | solution.py:60
  341.7 5.4 copy-start.2
  341.8 7.1 %copy-start.8 = (bf16[1536,3072]{1,0:T(8,128)(2,1)S(1)}, bf16[1536,3072]{1,0:T(8,128)(2,1)}, u32[]{:S(2)}) copy-start(bf16[1536,3072]{1,0:T(8,128)(2,1)} %all-gather.2.cloned.1.call-done) | copy-start | bytes 28311556
Sparse Core Ops, SparseCore 0:
  59.7 277.0 reduce-scatter.6
  343.5 226.4 all-reduce.1
Sparse Core Ops, SparseCore 1:
  62.6 147.1 all-gather.1
  339.6 77.7 reduce-scatter.4
where the time goes:
time: 580 us; the launch traced here: 579 us
  waiting for transfers between devices  493 us (85%)
  local copies, waits for them, and re-layouts  25.1 us (4%)
  blocking collectives  22.1 us (4%)
  matrix products  21.5 us (4%)
  between operations  17.8 us (3%)
    unnamed x5, waiting for transfers between devices  277 us
    psum x1, waiting for transfers between devices, local(): grad_embed = lax.psum(embed_term, 'seq')  151 us
    reduce_scatter x1, waiting for transfers between devices, local(): grad_w = lax.psum_scatter(row_sums, 'clip', scatter_dimension=1, tiled=True)  64.7 us
    unnamed x22, local copies, waits for them, and re-layouts  25.1 us
    psum x1, blocking collectives, local(): reward_sum = lax.psum(rewards, 'clip')  22.1 us
  transfers between devices with their start and end apart: 4, of which 3 were waited for; matrix products, arithmetic and copies ran while one was open for 3% of the time, Pallas kernels for 0%

commit v1 on v0

v1 whole, which is shorter than its diff:
```python
import jax
import jax.numpy as jnp
from jax import lax
from jax.experimental import pallas as pl
from jax.experimental.pallas import tpu as pltpu
from jax.sharding import PartitionSpec as P

NSTEPS = 16
SHIFT_FACTOR = 7.0
GUIDANCE = 6.0
NOISE_LEVEL = 0.3

D = 3072
H = 1536
CH = 64
TOK = 256
NX, NZ = 4, 8
CLIPS = 8
SL = D // CLIPS
HALF = H // 2
ROWS = 48
ZROWS = 2 * ROWS
NC = 4
CC = D // NC
TILE = 256
MESH = pl.DeviceIdType.MESH
F32, BF16 = jnp.float32, jnp.bfloat16


def sigma_level(index):
    tval = 1.0 - index.astype(F32) / NSTEPS
    return SHIFT_FACTOR * tval / (1.0 + (SHIFT_FACTOR - 1.0) * tval)


def dev(x, h, lo, z, core):
    return (h * NX + x, z * 4 + lo * 2 + core)


def kernel(
    step_ref, rew_ref, lat_ref, noi_ref, vc_ref, vu_ref, ew_ref, gate_ref, vals_ref, w_ref, cot_ref,
    bo_ref, ga_ref, gw_ref, ge_ref,
    vals_v, cot2, a2, vts, wf, gs, es, zls, zlr, zss, zsr, fs, fr, e1s, e1r, e2s, e2r, ef,
    rsb, rrb, samp_t, branch, gadv, advb, ga_acc,
    loc, r_s, r_r, cot_s, cot_r, a2_s, a2_r, wx_s, wy_s, wc_s, w_r, wc_r,
    zl_s, zl_r, zs_s, zs_r, f_s, f_r, e1_s, e1_r, e2_s, e2_r, e3_s, e3_r, e4_s, e4_r,
):
    clip = lax.axis_index("clip")
    seq = lax.axis_index("seq")
    h, x = lax.div(clip, NX), lax.rem(clip, NX)
    z, lo, core = lax.div(seq, 4), lax.rem(lax.div(seq, 2), 2), lax.rem(seq, 2)
    oc, olo, oh = 1 - core, 1 - lo, 1 - h
    sgn = 1 - 2 * core

    def xr(n):
        return lax.rem(x + n + NX, NX)

    def zr(n):
        return lax.rem(z + n + NZ, NZ)

    def rcopy(src, dst, ss, rs, to):
        return pltpu.make_async_remote_copy(
            src_ref=src, dst_ref=dst, send_sem=ss, recv_sem=rs, device_id=to, device_id_type=MESH
        )

    ld_vals = pltpu.make_async_copy(vals_ref, vals_v, loc.at[0])
    ld_cot = pltpu.make_async_copy(cot_ref, cot2.at[pl.ds(0, TOK)], loc.at[1])
    ld_w0 = pltpu.make_async_copy(w_ref.at[pl.ds(0, HALF)], wf.at[clip, 0], loc.at[2])
    ld_w1 = pltpu.make_async_copy(w_ref.at[pl.ds(HALF, HALF)], wf.at[clip, 1], loc.at[3])
    ld_vals.start()
    ld_cot.start()
    ld_w0.start()
    ld_w1.start()

    bar = pltpu.get_barrier_semaphore()
    me16 = clip * 2 + lo
    partners = []
    for r in range(1, 16):
        o = lax.rem(me16 + r, 16)
        oclip, olo_ = lax.div(o, 2), lax.rem(o, 2)
        partners.append((oclip, z * 4 + olo_ * 2 + core))
    for r in range(1, NZ):
        partners.append(dev(x, h, lo, zr(r), core))
    partners.append(dev(x, h, lo, z, oc))
    partners.append(dev(x, h, olo, z, oc))
    for p in partners:
        pl.semaphore_signal(bar, inc=1, device_id=p, device_id_type=MESH)

    rsb[...] = jnp.full((8, 128), rew_ref[0], F32)
    rrb[clip] = jnp.full((8, 128), rew_ref[0], F32)
    idx = jnp.full((1, TOK), step_ref[0], jnp.int32)
    sig_now = sigma_level(idx)
    sig_next = sigma_level(idx + 1)
    uncond = vu_ref[...].astype(F32)
    guided = uncond + GUIDANCE * (vc_ref[...].astype(F32) - uncond)
    spread = NOISE_LEVEL * jnp.sqrt(sig_now - sig_next)
    sampled = lat_ref[...] + (sig_next - sig_now) * guided + spread * noi_ref[...]
    samp_t[...] = sampled.T.astype(BF16)
    samp_b = sampled.astype(BF16)
    vts[0, pl.ds(HALF, 32), :] = samp_b[0:32]
    vts[1, pl.ds(HALF, 32), :] = samp_b[32:64]

    pl.semaphore_wait(bar, len(partners))

    rsends = []
    for r in range(1, CLIPS):
        c = lax.rem(clip + r, CLIPS)
        cp = rcopy(rsb, rrb.at[clip], r_s.at[r - 1], r_r.at[clip], (c, seq))
        cp.start()
        rsends.append(cp)
    core_dev = dev(x, h, lo, z, oc)
    cp_cot = rcopy(cot_ref, cot2.at[pl.ds(TOK, TOK)], cot_s, cot_r, core_dev)
    cp_cot.start()

    role_c = core == olo
    role_r = core == lo
    side = dev(x, h, olo, z, core)
    cross = dev(x, oh, olo, z, core)
    own_half = w_ref.at[pl.ds(pl.multiple_of(core * HALF, HALF), HALF)]

    def w_own(ss, to):
        return rcopy(own_half, wf.at[clip, core], ss, w_r.at[clip], to)

    def w_fwd(slot, ss, to):
        return rcopy(wf.at[slot, core], wf.at[slot, core], ss, w_r.at[slot], to)

    xp = dev(xr(1), h, lo, z, core)
    xm = dev(xr(-1), h, lo, z, core)
    w_own(wx_s.at[0], xp).start()
    w_own(wx_s.at[1], xm).start()

    @pl.when(role_c)
    def _():
        w_own(wy_s.at[0], cross).start()

    def a_slot(i):
        return h * NX + xr(i)

    def b_slot(i):
        return oh * NX + xr(i)

    def w_core(slot):
        return rcopy(wf.at[slot, core], wf.at[slot, core], wc_s.at[slot], wc_r.at[slot], core_dev)

    def w_core_other(slot):
        return rcopy(wf.at[slot, oc], wf.at[slot, oc], wc_s.at[slot], wc_r.at[slot], core_dev)

    def got(slot):
        w_fwd(slot, wx_s.at[0], xp).wait_recv()
        w_core(slot).start()

    ld_vals.wait()
    for b in range(H // 384):
        vt = vals_v[:, b * 384:(b + 1) * 384].T
        for q in range(8):
            s = b * 8 + q
            zz, ll, cc = s // 4, (s // 2) % 2, s % 2
            vts[cc, pl.ds(zz * ZROWS + ll * ROWS, ROWS), :] = vt[q * ROWS:(q + 1) * ROWS]
    cp_a2 = rcopy(vts.at[oc], a2.at[:, pl.ds(TOK, TOK)], a2_s, a2_r, core_dev)
    cp_a2.start()
    a2[:, pl.ds(0, TOK)] = vts[core]

    for r in range(1, CLIPS):
        c = lax.rem(clip + r, CLIPS)
        rcopy(rsb, rrb.at[c], r_s.at[r - 1], r_r.at[c], (c, seq)).wait_recv()
    total = rrb[0]
    for c in range(1, CLIPS):
        total = total + rrb[c]
    adv = rrb[clip] - total / CLIPS
    advb[...] = adv
    adv1 = adv[0:1, 0:1]
    gadv[...] = gate_ref[...] * adv1

    ld_cot.wait()
    cp_cot.wait_recv()
    cp_a2.wait_recv()

    zl_dev = dev(x, h, lo, zr(sgn), core)
    zs_dev = dev(x, h, lo, zr(-sgn), core)

    def zlong(t, k):
        return rcopy(zls.at[t, k], zlr.at[t, k], zl_s.at[t * NC + k], zl_r.at[t * NC + k], zl_dev)

    def zshort(t, k):
        return rcopy(zss.at[t, k], zsr.at[t, k], zs_s.at[t * NC + k], zs_r.at[t * NC + k], zs_dev)

    def block(k, d):
        return gs[k, pl.ds(pl.multiple_of(d * ZROWS, ZROWS), ZROWS), :]

    def zstep(t, k):
        d = zr(sgn * (4 - t))
        if t == 0:
            zls[t, k] = block(k, d).astype(BF16)
        else:
            zlong(t - 1, k).wait_recv()
            zls[t, k] = (block(k, d) + zlr[t - 1, k].astype(F32)).astype(BF16)
        zlong(t, k).start()
        if t < 3:
            d = zr(-sgn * (3 - t))
            if t == 0:
                zss[t, k] = block(k, d).astype(BF16)
            else:
                zshort(t - 1, k).wait_recv()
                zss[t, k] = (block(k, d) + zsr[t - 1, k].astype(F32)).astype(BF16)
            zshort(t, k).start()

    def g_chunk(k):
        def tile(j, carry):
            off = pl.multiple_of(j * TILE, TILE)
            cols = pl.ds(pl.multiple_of(k * CC + j * TILE, TILE), TILE)
            g = jnp.dot(a2[...], cot2[:, cols], preferred_element_type=F32)
            gs[k, :, pl.ds(off, TILE)] = g[:HALF] * gadv[:, cols]
            es[:, cols] = g[HALF:] * advb[0:1, 0:1]
            return carry
        lax.fori_loop(0, CC // TILE, tile, 0)

    def f_copy(q):
        to = (q // 2, z * 4 + (q % 2) * 2 + core)
        return rcopy(fs.at[q], fr.at[me16], f_s.at[q], f_r.at[me16], to)

    def final(k):
        zlong(3, k).wait_recv()
        zshort(2, k).wait_recv()
        r = block(k, z) + zlr[3, k].astype(F32) + zsr[2, k].astype(F32)
        for j in range(2):
            for l in range(2):
                q = (2 * k + j) * 2 + l
                fs[q] = r[l * ROWS:(l + 1) * ROWS, j * SL:(j + 1) * SL].astype(BF16)

                @pl.when(me16 != q)
                def _():
                    f_copy(q).start()

    def w_use(slot, first=False, own=False):
        if own:
            ld_w0.wait()
            ld_w1.wait()
        else:
            w_core_other(slot).wait_recv()
        cols = pl.ds(pl.multiple_of(slot * SL, SL), SL)
        proj = jnp.dot(vals_v[:, :HALF], wf[slot, 0], preferred_element_type=F32)
        proj = proj + jnp.dot(vals_v[:, HALF:], wf[slot, 1], preferred_element_type=F32)
        emb = jnp.dot(samp_t[...], ew_ref[:, cols], preferred_element_type=F32)
        bo_ref[:, cols] = (emb + gate_ref[:, cols] * proj).astype(BF16)
        br = branch[:, cols]
        for i in range(2):
            g = lax.dot_general(br, wf[slot, i], (((1,), (1,)), ((), ())), preferred_element_type=F32)
            if first:
                ga_acc[:, i * HALF:(i + 1) * HALF] = g
            else:
                ga_acc[:, i * HALF:(i + 1) * HALF] += g

    me4 = core * 2 + lo

    def e1_copy():
        return rcopy(e1s, e1r, e1_s, e1_r, side)

    def e2_copy(r):
        return rcopy(e2s.at[zr(r)], e2r.at[z], e2_s.at[r - 1], e2_r.at[z], dev(x, h, lo, zr(r), core))

    def e3_copy(r):
        return rcopy(ef.at[me4, z], ef.at[me4, z], e3_s.at[r - 1], e3_r.at[z], dev(x, h, lo, zr(r), core))

    def e4_copy(i):
        to = [side, core_dev, dev(x, h, olo, z, oc)][i]
        return rcopy(ef.at[me4], ef.at[me4], e4_s.at[i], e4_r.at[me4], to)

    def e_one():
        e1s[...] = es[pl.ds(pl.multiple_of(olo * 16, 16), 16), :].astype(BF16)
        e1_copy().start()

    def e_two():
        e1_copy().wait_recv()
        part = es[pl.ds(pl.multiple_of(lo * 16, 16), 16), :] + e1r[...].astype(F32)
        for d in range(NZ):
            e2s[d] = part[:, d * SL:(d + 1) * SL].astype(BF16)
        for r in range(1, NZ):
            e2_copy(r).start()
        e2r[z] = e2s[z]

    def e_three():
        for r in range(1, NZ):
            o = zr(r)
            rcopy(e2s.at[o], e2r.at[o], e2_s.at[r - 1], e2_r.at[o], dev(x, h, lo, o, core)).wait_recv()
        tot = e2r[0].astype(F32)
        for d in range(1, NZ):
            tot = tot + e2r[d].astype(F32)
        ef[me4, z] = tot.astype(BF16)
        for r in range(1, NZ):
            e3_copy(r).start()

    def e_four():
        for r in range(1, NZ):
            o = zr(r)
            rcopy(ef.at[me4, o], ef.at[me4, o], e3_s.at[r - 1], e3_r.at[o], dev(x, h, lo, o, core)).wait_recv()
        for i in range(3):
            e4_copy(i).start()

    def e_five():
        for i, q in enumerate((core * 2 + olo, oc * 2 + lo, oc * 2 + olo)):
            rcopy(ef.at[q], ef.at[q], e4_s.at[i], e4_r.at[q], side).wait_recv()
        for q in range(4):
            for d in range(NZ):
                ge_ref[q * 16:(q + 1) * 16, d * SL:(d + 1) * SL] = ef[q, d].astype(F32)

    def y_c(i):
        w_fwd(a_slot(i), wy_s.at[i], cross).start()

    def y_r(i):
        got(b_slot(i))
        w_fwd(b_slot(i), wy_s.at[i], side).start()

    def stage_xa():
        got(a_slot(1))
        got(a_slot(3))
        w_fwd(h * NX + xr(-sgn), wx_s.at[2], dev(xr(sgn), h, lo, z, core)).start()

        @pl.when(role_c)
        def _():
            y_c(1)
            y_c(3)

    def stage_xb():
        got(a_slot(2))

        @pl.when(role_c)
        def _():
            y_c(2)

    def stage_r(i):
        @pl.when(role_r)
        def _():
            y_r(i)

    def stage_c(i):
        @pl.when(role_c)
        def _():
            got(b_slot(i))

    for k in range(NC):
        g_chunk(k)
        zstep(0, k)
    e_one()
    stage_r(0)
    scaled = (cot2[pl.ds(0, TOK), :].astype(F32) * advb[0:1, 0:1]).astype(BF16)
    branch[...] = (scaled.astype(F32) * gate_ref[...]).astype(BF16)

    zstep(1, 0)
    e_two()
    w_use(clip, first=True, own=True)
    zstep(1, 1)
    stage_xa()
    stage_c(0)
    zstep(1, 2)
    w_use(b_slot(0))
    e_three()
    zstep(1, 3)
    w_use(a_slot(1))
    zstep(2, 0)
    stage_xb()
    stage_r(1)
    w_use(a_slot(3))
    zstep(2, 1)
    e_four()
    w_use(a_slot(2))
    zstep(2, 2)
    stage_r(3)
    stage_c(1)
    zstep(2, 3)
    e_five()
    w_use(b_slot(1))
    zstep(3, 0)
    stage_r(2)
    stage_c(3)
    zstep(3, 1)
    w_use(b_slot(3))
    zstep(3, 2)
    stage_c(2)
    zstep(3, 3)
    w_use(b_slot(2))
    ga_ref[...] = ga_acc[...].astype(BF16)
    for k in range(NC):
        final(k)

    for q in range(16):
        @pl.when(me16 == q)
        def _():
            fr[q] = fs[q]

        @pl.when(me16 != q)
        def _():
            rcopy(fs.at[q], fr.at[q], f_s.at[q], f_r.at[q], core_dev).wait_recv()
    acc = fr[0].astype(F32)
    for q in range(1, 16):
        acc = acc + fr[q].astype(F32)
    gw_ref[...] = acc

    for cp in rsends:
        cp.wait_send()
    cp_cot.wait_send()
    cp_a2.wait_send()
    w_own(wx_s.at[0], xp).wait_send()
    w_own(wx_s.at[1], xm).wait_send()
    w_fwd(a_slot(1), wx_s.at[2], xp).wait_send()
    for i in range(4):
        w_fwd(a_slot(1), wy_s.at[i], side).wait_send()
    for i in range(1, 4):
        w_core(a_slot(i)).wait_send()
    for i in range(4):
        w_core(b_slot(i)).wait_send()
    for t in range(4):
        for k in range(NC):
            zlong(t, k).wait_send()
            if t < 3:
                zshort(t, k).wait_send()
    for q in range(16):
        @pl.when(me16 != q)
        def _():
            f_copy(q).wait_send()
    e1_copy().wait_send()
    for r in range(1, NZ):
        e2_copy(r).wait_send()
        e3_copy(r).wait_send()
    for i in range(3):
        e4_copy(i).wait_send()


def fused(step, rewards, lat, noi, vc, vu, ew, gate, vals, w, cot):
    vm = pl.BlockSpec(memory_space=pltpu.VMEM)
    sm = pl.BlockSpec(memory_space=pltpu.SMEM)
    anyspace = pl.BlockSpec(memory_space=pl.ANY)
    dma = pltpu.SemaphoreType.DMA
    scratch = [
        pltpu.VMEM((TOK, H), BF16),
        pltpu.VMEM((2 * TOK, D), BF16),
        pltpu.VMEM((HALF + 32, 2 * TOK), BF16),
        pltpu.VMEM((2, HALF + 32, TOK), BF16),
        pltpu.VMEM((CLIPS, 2, HALF, SL), BF16),
        pltpu.VMEM((NC, HALF, CC), F32),
        pltpu.VMEM((32, D), F32),
        pltpu.VMEM((4, NC, ZROWS, CC), BF16),
        pltpu.VMEM((4, NC, ZROWS, CC), BF16),
        pltpu.VMEM((3, NC, ZROWS, CC), BF16),
        pltpu.VMEM((3, NC, ZROWS, CC), BF16),
        pltpu.VMEM((16, ROWS, SL), BF16),
        pltpu.VMEM((16, ROWS, SL), BF16),
        pltpu.VMEM((16, D), BF16),
        pltpu.VMEM((16, D), BF16),
        pltpu.VMEM((NZ, 16, SL), BF16),
        pltpu.VMEM((NZ, 16, SL), BF16),
        pltpu.VMEM((4, NZ, 16, SL), BF16),
        pltpu.VMEM((8, 128), F32),
        pltpu.VMEM((CLIPS, 8, 128), F32),
        pltpu.VMEM((TOK, CH), BF16),
        pltpu.VMEM((TOK, D), BF16),
        pltpu.VMEM((1, D), F32),
        pltpu.VMEM((8, 128), F32),
        pltpu.VMEM((TOK, H), F32),
        dma((4,)), dma((7,)), dma((8,)), dma, dma, dma, dma,
        dma((3,)), dma((4,)), dma((8,)), dma((8,)), dma((8,)),
        dma((4 * NC,)), dma((4 * NC,)), dma((3 * NC,)), dma((3 * NC,)),
        dma((16,)), dma((16,)), dma, dma,
        dma((7,)), dma((8,)), dma((7,)), dma((8,)), dma((3,)), dma((4,)),
    ]
    return pl.pallas_call(
        kernel,
        name="fused_step",
        out_shape=(
            jax.ShapeDtypeStruct((TOK, D), BF16),
            jax.ShapeDtypeStruct((TOK, H), BF16),
            jax.ShapeDtypeStruct((ROWS, SL), F32),
            jax.ShapeDtypeStruct((CH, D), F32),
        ),
        in_specs=[sm, sm, vm, vm, vm, vm, vm, vm, anyspace, anyspace, anyspace],
        out_specs=(vm, vm, vm, vm),
        scratch_shapes=scratch,
        compiler_params=pltpu.CompilerParams(
            collective_id=0, has_side_effects=True, vmem_limit_bytes=58 * 2**20
        ),
    )(step, rewards, lat, noi, vc, vu, ew, gate, vals, w, cot)


def local(latent, sample_noise, vel_cond, vel_uncond, step_index, embed_w, gate_scale, attn_vals, out_w, cotangent, rewards):
    bo, ga, gw, ge = fused(
        step_index, rewards, latent[0], sample_noise[0], vel_cond[0], vel_uncond[0], embed_w,
        gate_scale, attn_vals[0], out_w, cotangent[0],
    )
    return bo[None], ga[None], gw, ge[None]


def solution(mesh):
    in_specs = (
        P("clip", None, "seq"),
        P("clip", None, "seq"),
        P("clip", None, "seq"),
        P("clip", None, "seq"),
        P(),
        P(),
        P("clip", None),
        P("clip", "seq", None),
        P(None, "clip"),
        P("clip", "seq", None),
        P("clip"),
    )
    out_specs = (
        P("clip", "seq", None),
        P("clip", "seq", None),
        P("seq", "clip"),
        P("clip", None, None),
    )
    return jax.shard_map(local, mesh=mesh, in_specs=in_specs, out_specs=out_specs, check_vma=False)
```

time: 580 us -> 87.1 us (0.15)
  waiting for transfers between devices: 493 us -> 0 us
  Pallas kernels: 0 us -> 79.8 us
  blocking collectives: 22.1 us -> 0 us
  matrix products: 21.5 us -> 0 us
  local copies, waits for them, and re-layouts: 25.1 us -> 5.15 us
  between operations: 17.8 us -> 1.95 us
    unnamed x5 -> x0, waiting for transfers between devices: 277 us -> none
    psum x1 -> x0, waiting for transfers between devices: 151 us -> none  [local(): grad_embed = lax.psum(embed_term, 'seq')]
    pallas_call x0 -> x1, Pallas kernels: none -> 79.8 us  [fused(): pl.pallas_call(kernel, name='fused_step', out_shape=(jax.ShapeDtypeStruct...]
    reduce_scatter x1 -> x0, waiting for transfers between devices: 64.7 us -> none  [local(): grad_w = lax.psum_scatter(row_sums, 'clip', scatter_dimension=1, tiled=True)]
    psum x1 -> x0, blocking collectives: 22.1 us -> none  [local(): reward_sum = lax.psum(rewards, 'clip')]
    dot_general x5 -> x0, matrix products: 21.5 us -> none  [the longest x1 9.41 us: local(): lax.dot_general(values, branch, contract_first, preferred_element_type=jn...]
    unnamed x22 -> x10, local copies, waits for them, and re-layouts: 25.1 us -> 5.15 us
  transfers between devices with their start and end apart: 4 -> 0, of which waited for: 3 -> 0; matrix products, arithmetic and copies ran while one was open for 3% -> 0% of each run, Pallas kernels for 0% -> 0%
where the time goes in v1:
time: 87.1 us; the launch traced here: 86.9 us
  Pallas kernels  79.8 us (92%)
  local copies, waits for them, and re-layouts  5.15 us (6%)
  between operations  1.95 us (2%)
    pallas_call x1, Pallas kernels, fused(): pl.pallas_call(kernel, name='fused_step', out_shape=(jax.ShapeDtypeStruct...  79.8 us
    unnamed x10, local copies, waits for them, and re-layouts  5.15 us

profile of v1, /device:TPU:1, one launch (start us, length us, event | category | flops | bytes accessed | tf_op | source)
XLA Modules:
  0.0 86.9 jit_solution(597443876340020324)
XLA Ops:
  1.9 79.8 %fused_step.1 = (bf16[256,3072]{1,0:T(8,128)(2,1)}, bf16[256,1536]{1,0:T(8,128)(2,1)}, f32[48,384]{1,0:T(8,128)}, f32[64,3072]{1,0:T(8,128)}) custom-call(s32[1]{0:T(128)S(6)} %copy.19.step_ref, f32[1]{0:T(128)S(6)} %copy.20.rew_ref, f32[64,256]{1,0:T(8,128)} %bitcast.14, f32[64,256]{1,0:T(8,128)} %bitcast.15, bf16[64,256]{1,0:T(8,128)(2,1)} %bitcast.16, ...), custom_call_target="tpu_custom_call" | custom-call | tf_op jit(solution)/shard_map/fused_step/pallas_call | solution.py:464
  81.8 0.0 copy-start.1
  81.8 2.7 %copy.21 = bf16[1,256,3072]{2,1,0:T(8,128)(2,1)} copy(bf16[1,256,3072]{2,1,0:T(8,128)(2,1)} %bitcast.9) | data formatting | bytes 3145728
  84.5 0.0 copy-done.1
  84.5 0.0 copy-start.2
  84.5 0.0 copy-start
  84.5 0.9 %copy.22 = bf16[1,256,1536]{2,1,0:T(8,128)(2,1)} copy(bf16[1,256,1536]{2,1,0:T(8,128)(2,1)S(1)} %bitcast.12) | data formatting | bytes 1572864
  85.4 0.0 copy-done.2
  85.4 0.6 copy.23
  86.1 0.0 copy-done
  86.1 0.9 %copy.24 = f32[1,64,3072]{2,1,0:T(8,128)} copy(f32[1,64,3072]{2,1,0:T(8,128)S(1)} %bitcast.11) | data formatting | bytes 1572864
Async XLA Ops:
  81.8 2.7 %copy-start.1 = (bf16[256,1536]{1,0:T(8,128)(2,1)S(1)}, bf16[256,1536]{1,0:T(8,128)(2,1)}, u32[]{:S(2)}) copy-start(bf16[256,1536]{1,0:T(8,128)(2,1)} %get-tuple-element.9) | copy-start | bytes 2359300
  84.5 0.9 %copy-start.2 = (f32[48,384]{1,0:T(8,128)S(1)}, f32[48,384]{1,0:T(8,128)}, u32[]{:S(2)}) copy-start(f32[48,384]{1,0:T(8,128)} %get-tuple-element.18) | copy-start | bytes 221188
  84.5 1.5 %copy-start = (f32[64,3072]{1,0:T(8,128)S(1)}, f32[64,3072]{1,0:T(8,128)}, u32[]{:S(2)}) copy-start(f32[64,3072]{1,0:T(8,128)} %get-tuple-element.11) | copy-start | bytes 2359300

commit v2 on v1

v2 whole, which is shorter than its diff:
```python
import jax
import jax.numpy as jnp
from jax import lax
from jax.experimental import pallas as pl
from jax.experimental.pallas import tpu as pltpu
from jax.sharding import PartitionSpec as P

NSTEPS = 16
SHIFT_FACTOR = 7.0
GUIDANCE = 6.0
NOISE_LEVEL = 0.3

D = 3072
H = 1536
CH = 64
TOK = 256
NX, NZ = 4, 8
CLIPS = 8
SL = D // CLIPS
HALF = H // 2
ROWS = 48
ZROWS = 2 * ROWS
NC = 4
CC = D // NC
TILE = 256
QR = H // 4
NARROW = 2 * SL // 3
THIRD = SL - NARROW
ZW = 2 * NARROW
SW = CLIPS * THIRD + 128
MESH = pl.DeviceIdType.MESH
F32, BF16 = jnp.float32, jnp.bfloat16


def sigma_level(index):
    tval = 1.0 - index.astype(F32) / NSTEPS
    return SHIFT_FACTOR * tval / (1.0 + (SHIFT_FACTOR - 1.0) * tval)


def dev(x, h, lo, z, core):
    return (h * NX + x, z * 4 + lo * 2 + core)


def kernel(
    step_ref, rew_ref, lat_ref, noi_ref, vc_ref, vu_ref, ew_ref, gate_ref, vals_ref, w_ref, cot_ref,
    bo_out, ga_out, gw_out, ge_out,
    vals_v, cot2, a2, vts, wf, gs, es, zls, zlr, zss, zsr, fs, fr, fss, frs, ef,
    sss, ssr, szls, szlr, szss, szsr,
    e_own, eo, er, gside, rsb, rrb, samp, samp_t, branch, gadv, advb, ga_acc, bo_ref, ga_ref, gw_ref, ge_ref,
    loc, r_s, r_r, cot_s, cot_r, a2_s, a2_r, wx_s, wy_s, wc_s, w_r, wc_r,
    ss_s, ss_r, szl_s, szl_r, szs_s, szs_r, zl_s, zl_r, zs_s, zs_r, f_s, f_r, f2_s, f2_r, e1_s, e1_r, e3_s, e3_r, e4_s, e4_r,
):
    clip = lax.axis_index("clip")
    seq = lax.axis_index("seq")
    h, x = lax.div(clip, NX), lax.rem(clip, NX)
    z, lo, core = lax.div(seq, 4), lax.rem(lax.div(seq, 2), 2), lax.rem(seq, 2)
    oc, olo, oh = 1 - core, 1 - lo, 1 - h
    sgn = 1 - 2 * core

    def xr(n):
        return lax.rem(x + n + NX, NX)

    def zr(n):
        return lax.rem(z + n + NZ, NZ)

    def rcopy(src, dst, ss, rs, to):
        return pltpu.make_async_remote_copy(
            src_ref=src, dst_ref=dst, send_sem=ss, recv_sem=rs, device_id=to, device_id_type=MESH
        )

    ld_vals = pltpu.make_async_copy(vals_ref, vals_v, loc.at[0])
    ld_cot = pltpu.make_async_copy(cot_ref, cot2.at[pl.ds(0, TOK)], loc.at[1])
    ld_w = pltpu.make_async_copy(w_ref, wf.at[clip], loc.at[2])
    ld_vals.start()
    ld_cot.start()
    ld_w.start()

    bar = pltpu.get_barrier_semaphore()
    me16 = clip * 2 + lo
    partners = []
    for r in range(1, 16):
        o = lax.rem(me16 + r, 16)
        oclip, olo_ = lax.div(o, 2), lax.rem(o, 2)
        partners.append((oclip, z * 4 + olo_ * 2 + core))
    for r in range(1, NZ):
        partners.append(dev(x, h, lo, zr(r), core))
    partners.append(dev(x, h, lo, z, oc))
    partners.append(dev(x, h, olo, z, oc))
    for p in partners:
        pl.semaphore_signal(bar, inc=1, device_id=p, device_id_type=MESH)

    rsb[...] = jnp.full((8, 128), rew_ref[0], F32)
    rrb[clip] = jnp.full((8, 128), rew_ref[0], F32)
    idx = jnp.full((1, TOK), step_ref[0], jnp.int32)
    sig_now = sigma_level(idx)
    sig_next = sigma_level(idx + 1)
    uncond = vu_ref[...].astype(F32)
    guided = uncond + GUIDANCE * (vc_ref[...].astype(F32) - uncond)
    spread = NOISE_LEVEL * jnp.sqrt(sig_now - sig_next)
    sampled = lat_ref[...] + (sig_next - sig_now) * guided + spread * noi_ref[...]
    samp_t[...] = sampled.T.astype(BF16)
    samp_b = sampled.astype(BF16)
    samp[...] = samp_b

    ld_vals.wait()
    for b in range(H // 384):
        vt = vals_v[:, b * 384:(b + 1) * 384].T
        for q in range(8):
            s = b * 8 + q
            zz, ll, cc = s // 4, (s // 2) % 2, s % 2
            vts[cc, pl.ds(zz * ZROWS + ll * ROWS, ROWS), :] = vt[q * ROWS:(q + 1) * ROWS]
    a2[:, pl.ds(0, TOK)] = vts[core]

    pl.semaphore_wait(bar, len(partners))

    core_dev = dev(x, h, lo, z, oc)
    cp_a2 = rcopy(vts.at[oc], a2.at[:, pl.ds(TOK, TOK)], a2_s, a2_r, core_dev)
    cp_a2.start()
    cp_cot = []
    for k in range(NC):
        cols = pl.ds(k * CC, CC)
        cp = rcopy(cot_ref.at[:, cols], cot2.at[pl.ds(TOK, TOK), cols], cot_s.at[k], cot_r.at[k], core_dev)
        cp.start()
        cp_cot.append(cp)
    rsends = []
    for r in range(1, CLIPS):
        c = lax.rem(clip + r, CLIPS)
        cp = rcopy(rsb, rrb.at[clip], r_s.at[r - 1], r_r.at[clip], (c, seq))
        cp.start()
        rsends.append(cp)

    side = dev(x, h, olo, z, core)
    cross = dev(x, oh, olo, z, core)

    def quarter(i):
        return pl.ds(pl.multiple_of((core * 2 + i) * QR, QR), QR)

    def w_own(i, ss, to):
        return rcopy(w_ref.at[quarter(i)], wf.at[clip, quarter(i)], ss, w_r.at[clip * 2 + i], to)

    def w_fwd(slot, i, ss, to):
        return rcopy(wf.at[slot, quarter(i)], wf.at[slot, quarter(i)], ss, w_r.at[slot * 2 + i], to)

    xp = dev(xr(1), h, lo, z, core)
    xm = dev(xr(-1), h, lo, z, core)
    xs = dev(xr(sgn), h, lo, z, core)
    for i in range(2):
        w_own(i, wx_s.at[2 * i], xp).start()
        w_own(i, wx_s.at[2 * i + 1], xm).start()
        w_own(i, wy_s.at[i], cross).start()

    def a_slot(i):
        return h * NX + xr(i)

    def b_slot(i):
        return oh * NX + xr(i)

    def w_core(slot, i):
        n = slot * 2 + i
        return rcopy(wf.at[slot, quarter(i)], wf.at[slot, quarter(i)], wc_s.at[n], wc_r.at[n], core_dev)

    def w_core_other(slot, i):
        n = slot * 2 + i
        rows = pl.ds(pl.multiple_of((oc * 2 + i) * QR, QR), QR)
        return rcopy(wf.at[slot, rows], wf.at[slot, rows], wc_s.at[n], wc_r.at[n], core_dev)

    def got(slot, i):
        w_fwd(slot, i, wx_s.at[0], xp).wait_recv()
        w_core(slot, i).start()

    ld_cot.wait()

    zl_dev = dev(x, h, lo, zr(sgn), core)
    zs_dev = dev(x, h, lo, zr(-sgn), core)

    def zlong(t, k):
        n = t * NC + k
        return rcopy(zls.at[t, k], zlr.at[t, k], zl_s.at[n], zl_r.at[n], zl_dev)

    def zshort(t, k):
        n = t * NC + k
        return rcopy(zss.at[t, k], zsr.at[t, k], zs_s.at[n], zs_r.at[n], zs_dev)

    def zrows(d):
        return pl.ds(pl.multiple_of(d * ZROWS, ZROWS), ZROWS)

    def zadd(t, k, d, out, got_ref):
        v = gs[k, zrows(d), :]
        if t:
            v = v + got_ref[t - 1, k].astype(F32)
        out[t, k] = v.astype(BF16)

    def zstep(t, k):
        if t:
            zlong(t - 1, k).wait_recv()
        zadd(t, k, zr(sgn * (4 - t)), zls, zlr)
        zlong(t, k).start()
        if t < 3:
            if t:
                zshort(t - 1, k).wait_recv()
            zadd(t, k, zr(-sgn * (3 - t)), zss, zsr)
            zshort(t, k).start()

    def lrows(d, l):
        return pl.ds(pl.multiple_of(d * ZROWS + l * ROWS, ROWS), ROWS)

    def sown(d, l):
        emb = []
        for i in range(3):
            cols = pl.ds(pl.multiple_of(d * SL + i * 128, 128), 128)
            emb.append(es[pl.ds(pl.multiple_of(l * 16, 16), 16), cols])
        return jnp.concatenate([gside[lrows(d, l), :], jnp.concatenate(emb, axis=0)], axis=1)

    sorder = (sgn * 4, -sgn * 3, sgn * 3, -sgn * 2, sgn * 2, -sgn, sgn, 0)

    me4 = core * 2 + lo

    def e3_copy(r):
        return rcopy(ef.at[me4, z], ef.at[me4, z], e3_s.at[r - 1], e3_r.at[z], dev(x, h, lo, zr(r), core))

    def e4_copy(i):
        to = [side, core_dev, dev(x, h, olo, z, oc)][i]
        return rcopy(ef.at[me4], ef.at[me4], e4_s.at[i], e4_r.at[me4], to)

    def fs_copy(j):
        return rcopy(fss.at[j], frs.at[clip], f2_s.at[j], f2_r.at[clip], (j, seq))

    def side_copy(i):
        return rcopy(sss.at[i], ssr.at[i], ss_s.at[i], ss_r.at[i], side)

    def side_send():
        for i, n in enumerate(sorder):
            sss[i] = sown(zr(n), olo).astype(BF16)
            side_copy(i).start()

    def slong(t):
        return rcopy(szls.at[t], szlr.at[t], szl_s.at[t], szl_r.at[t], zl_dev)

    def sshort(t):
        return rcopy(szss.at[t], szsr.at[t], szs_s.at[t], szs_r.at[t], zs_dev)

    def sstep(t):
        side_copy(2 * t).wait_recv()
        v = sown(zr(sgn * (4 - t)), lo) + ssr[2 * t].astype(F32)
        if t:
            slong(t - 1).wait_recv()
            v = v + szlr[t - 1].astype(F32)
        szls[t] = v.astype(BF16)
        slong(t).start()
        if t < 3:
            side_copy(2 * t + 1).wait_recv()
            v = sown(zr(-sgn * (3 - t)), lo) + ssr[2 * t + 1].astype(F32)
            if t:
                sshort(t - 1).wait_recv()
                v = v + szsr[t - 1].astype(F32)
            szss[t] = v.astype(BF16)
            sshort(t).start()

    def sfinal():
        side_copy(7).wait_recv()
        slong(3).wait_recv()
        sshort(2).wait_recv()
        v = sown(z, lo) + ssr[7].astype(F32) + szlr[3].astype(F32) + szsr[2].astype(F32)
        for j in range(CLIPS):
            o = j * SL + NARROW
            fss[j] = (v[:, j * THIRD:(j + 1) * THIRD] * gadv[:, o:o + THIRD]).astype(BF16)

            @pl.when(clip != j)
            def _():
                fs_copy(j).start()
        emb = v[:, CLIPS * THIRD:].astype(BF16)
        ef[me4, z] = jnp.concatenate([emb[i * 16:(i + 1) * 16] for i in range(3)], axis=1)
        for r in range(1, NZ):
            e3_copy(r).start()

    def advantage():
        for r in range(1, CLIPS):
            c = lax.rem(clip + r, CLIPS)
            rcopy(rsb, rrb.at[c], r_s.at[r - 1], r_r.at[c], (c, seq)).wait_recv()
        total = rrb[0]
        for c in range(1, CLIPS):
            total = total + rrb[c]
        adv = rrb[clip] - total / CLIPS
        advb[...] = adv
        adv1 = adv[0:1, 0:1]
        gadv[...] = gate_ref[...] * adv1

    def e_first():
        def tile(j, carry):
            cols = pl.ds(pl.multiple_of(j * TILE, TILE), TILE)
            g = jnp.dot(samp[...], cot2[pl.ds(0, TOK), cols], preferred_element_type=F32)
            e_own[:, cols] = g
            eo[:, cols] = g.astype(BF16)
            return carry
        lax.fori_loop(0, D // TILE, tile, 0)
        e1_copy().start()

    def e1_copy():
        rows = pl.ds(pl.multiple_of(oc * 32, 32), 32)
        return rcopy(eo.at[rows], er, e1_s, e1_r, core_dev)

    def e_sum():
        e1_copy().wait_recv()
        es[...] = e_own[pl.ds(pl.multiple_of(core * 32, 32), 32), :] + er[...].astype(F32)

    def g_chunk(k):
        def tile(j, carry):
            cols = pl.ds(pl.multiple_of((2 * k + j) * SL, 128), NARROW)
            g = jnp.dot(a2[...], cot2[:, cols], preferred_element_type=F32)
            gs[k, :, pl.ds(pl.multiple_of(j * NARROW, NARROW), NARROW)] = g
            return carry
        lax.fori_loop(0, 2, tile, 0)

    def g_side():
        def tile(j, carry):
            parts = [cot2[:, pl.ds(pl.multiple_of((2 * j + i) * SL + NARROW, 128), THIRD)] for i in range(2)]
            g = jnp.dot(a2[...], jnp.concatenate(parts, axis=1), preferred_element_type=F32)
            gside[:, pl.ds(pl.multiple_of(j * 2 * THIRD, 2 * THIRD), 2 * THIRD)] = g
            return carry
        lax.fori_loop(0, NC, tile, 0)

    def f_copy(q):
        to = (q // 2, z * 4 + (q % 2) * 2 + core)
        return rcopy(fs.at[q], fr.at[me16], f_s.at[q], f_r.at[me16], to)

    def final(k):
        zlong(3, k).wait_recv()
        zshort(2, k).wait_recv()
        both = gs[k, zrows(z), :] + zlr[3, k].astype(F32) + zsr[2, k].astype(F32)
        for j in range(2):
            r = both[:, j * NARROW:(j + 1) * NARROW] * gadv[:, k * CC + j * SL:k * CC + j * SL + NARROW]
            for l in range(2):
                q = (2 * k + j) * 2 + l
                fs[q] = r[l * ROWS:(l + 1) * ROWS].astype(BF16)

                @pl.when(me16 != q)
                def _():
                    f_copy(q).start()

    def w_use(slot, first=False, own=False):
        if own:
            ld_w.wait()
        else:
            w_core_other(slot, 0).wait_recv()
            w_core_other(slot, 1).wait_recv()
        cols = pl.ds(pl.multiple_of(slot * SL, SL), SL)
        proj = jnp.dot(vals_v[...], wf[slot], preferred_element_type=F32)
        emb = jnp.dot(samp_t[...], ew_ref[:, cols], preferred_element_type=F32)
        bo_ref[:, cols] = (emb + gate_ref[:, cols] * proj).astype(BF16)
        br = branch[:, cols]
        for i in range(2):
            g = lax.dot_general(br, wf[slot, i * HALF:(i + 1) * HALF], (((1,), (1,)), ((), ())), preferred_element_type=F32)
            if first:
                ga_acc[:, i * HALF:(i + 1) * HALF] = g
            else:
                ga_acc[:, i * HALF:(i + 1) * HALF] += g

    def e_four():
        for r in range(1, NZ):
            o = zr(r)
            rcopy(ef.at[me4, o], ef.at[me4, o], e3_s.at[r - 1], e3_r.at[o], dev(x, h, lo, o, core)).wait_recv()
        for i in range(3):
            e4_copy(i).start()

    def e_five():
        for i, q in enumerate((core * 2 + olo, oc * 2 + lo, oc * 2 + olo)):
            rcopy(ef.at[q], ef.at[q], e4_s.at[i], e4_r.at[q], side).wait_recv()
        for q in range(4):
            for d in range(NZ):
                ge_ref[q * 16:(q + 1) * 16, d * SL:(d + 1) * SL] = ef[q, d].astype(F32) * advb[0:1, 0:1]
        pltpu.make_async_copy(ge_ref, ge_out, loc.at[4]).start()

    def stage_1():
        got(a_slot(1), 0)
        got(a_slot(3), 0)
        w_fwd(h * NX + xr(-sgn), 0, wx_s.at[4], xs).start()
        w_fwd(a_slot(1), 0, wy_s.at[2], cross).start()
        w_fwd(a_slot(3), 0, wy_s.at[3], cross).start()

    def stage_2():
        got(a_slot(1), 1)
        got(a_slot(3), 1)
        w_fwd(h * NX + xr(-sgn), 1, wx_s.at[5], xs).start()

    def stage_2b():
        got(b_slot(0), 0)
        got(b_slot(0), 1)
        w_fwd(b_slot(0), 1, wx_s.at[6], xp).start()
        w_fwd(b_slot(0), 1, wx_s.at[7], xm).start()

    def stage_3():
        got(a_slot(2), 0)
        w_fwd(a_slot(2), 0, wy_s.at[4], cross).start()

    def stage_4():
        got(a_slot(2), 1)

    def stage_5(i):
        got(b_slot(i), 0)

    def stage_6():
        got(b_slot(1), 1)
        got(b_slot(3), 1)
        w_fwd(oh * NX + xr(-sgn), 1, wx_s.at[8], xs).start()

    def stage_8():
        got(b_slot(2), 1)

    e_first()
    cp_a2.wait_recv()
    cp_cot[0].wait_recv()
    g_chunk(0)
    zstep(0, 0)
    for k in range(1, NC):
        cp_cot[k].wait_recv()
    g_side()
    e_sum()
    side_send()
    for k in range(1, NC):
        g_chunk(k)
        zstep(0, k)
    zstep(1, 0)
    stage_1()
    advantage()
    scaled = (cot2[pl.ds(0, TOK), :].astype(F32) * advb[0:1, 0:1]).astype(BF16)
    branch[...] = (scaled.astype(F32) * gate_ref[...]).astype(BF16)
    sstep(0)
    zstep(1, 1)
    zstep(1, 2)
    stage_2()
    stage_2b()
    w_use(clip, first=True, own=True)
    zstep(1, 3)
    stage_3()
    w_use(a_slot(1))
    zstep(2, 0)
    stage_5(1)
    w_use(a_slot(3))
    sstep(1)
    zstep(2, 1)
    stage_4()
    w_use(b_slot(0))
    zstep(2, 2)
    w_use(a_slot(2))
    zstep(2, 3)
    zstep(3, 0)
    stage_5(3)
    stage_6()
    w_use(b_slot(1))
    sstep(2)
    zstep(3, 1)
    stage_5(2)
    stage_8()
    w_use(b_slot(3))
    zstep(3, 2)
    zstep(3, 3)
    w_use(b_slot(2))
    pltpu.make_async_copy(bo_ref, bo_out, loc.at[6]).start()
    ga_ref[...] = ga_acc[...].astype(BF16)
    pltpu.make_async_copy(ga_ref, ga_out, loc.at[7]).start()
    final(0)
    sstep(3)
    final(1)
    final(2)
    final(3)
    sfinal()
    e_four()
    e_five()

    fr[me16] = fs[me16]
    frs[clip] = fss[clip]
    for q in range(16):
        @pl.when(me16 != q)
        def _():
            rcopy(fs.at[q], fr.at[q], f_s.at[q], f_r.at[q], core_dev).wait_recv()
    for j in range(CLIPS):
        @pl.when(clip != j)
        def _():
            rcopy(fss.at[j], frs.at[j], f2_s.at[j], f2_r.at[j], core_dev).wait_recv()
    acc = fr[0].astype(F32)
    for q in range(1, 16):
        acc = acc + fr[q].astype(F32)
    gw_ref[:, :NARROW] = acc
    acc = frs[0].astype(F32)
    for j in range(1, CLIPS):
        acc = acc + frs[j].astype(F32)
    gw_ref[:, NARROW:] = acc
    pltpu.make_async_copy(gw_ref, gw_out, loc.at[5]).start()

    pltpu.make_async_copy(ge_ref, ge_out, loc.at[4]).wait()
    pltpu.make_async_copy(gw_ref, gw_out, loc.at[5]).wait()
    pltpu.make_async_copy(bo_ref, bo_out, loc.at[6]).wait()
    pltpu.make_async_copy(ga_ref, ga_out, loc.at[7]).wait()
    for cp in rsends:
        cp.wait_send()
    for cp in cp_cot:
        cp.wait_send()
    cp_a2.wait_send()
    for n in range(9):
        w_fwd(a_slot(1), 0, wx_s.at[n], xp).wait_send()
    for n in range(5):
        w_fwd(a_slot(1), 0, wy_s.at[n], side).wait_send()
    for i in range(2):
        for n in range(1, 4):
            w_core(a_slot(n), i).wait_send()
        for n in range(4):
            w_core(b_slot(n), i).wait_send()
    for i in range(NZ):
        side_copy(i).wait_send()
    for t in range(4):
        slong(t).wait_send()
        if t < 3:
            sshort(t).wait_send()
        for k in range(NC):
            zlong(t, k).wait_send()
            if t < 3:
                zshort(t, k).wait_send()
    for q in range(16):
        @pl.when(me16 != q)
        def _():
            f_copy(q).wait_send()
    for j in range(CLIPS):
        @pl.when(clip != j)
        def _():
            fs_copy(j).wait_send()
    e1_copy().wait_send()
    for r in range(1, NZ):
        e3_copy(r).wait_send()
    for i in range(3):
        e4_copy(i).wait_send()


def fused(step, rewards, lat, noi, vc, vu, ew, gate, vals, w, cot):
    vm = pl.BlockSpec(memory_space=pltpu.VMEM)
    sm = pl.BlockSpec(memory_space=pltpu.SMEM)
    anyspace = pl.BlockSpec(memory_space=pl.ANY)
    dma = pltpu.SemaphoreType.DMA
    scratch = [
        pltpu.VMEM((TOK, H), BF16),
        pltpu.VMEM((2 * TOK, D), BF16),
        pltpu.VMEM((HALF, 2 * TOK), BF16),
        pltpu.VMEM((2, HALF, TOK), BF16),
        pltpu.VMEM((CLIPS, H, SL), BF16),
        pltpu.VMEM((NC, HALF, ZW), F32),
        pltpu.VMEM((32, D), F32),
        pltpu.VMEM((4, NC, ZROWS, ZW), BF16),
        pltpu.VMEM((4, NC, ZROWS, ZW), BF16),
        pltpu.VMEM((3, NC, ZROWS, ZW), BF16),
        pltpu.VMEM((3, NC, ZROWS, ZW), BF16),
        pltpu.VMEM((16, ROWS, NARROW), BF16),
        pltpu.VMEM((16, ROWS, NARROW), BF16),
        pltpu.VMEM((CLIPS, ROWS, THIRD), BF16),
        pltpu.VMEM((CLIPS, ROWS, THIRD), BF16),
        pltpu.VMEM((4, NZ, 16, SL), BF16),
        pltpu.VMEM((NZ, ROWS, SW), BF16),
        pltpu.VMEM((NZ, ROWS, SW), BF16),
        pltpu.VMEM((4, ROWS, SW), BF16),
        pltpu.VMEM((4, ROWS, SW), BF16),
        pltpu.VMEM((3, ROWS, SW), BF16),
        pltpu.VMEM((3, ROWS, SW), BF16),
        pltpu.VMEM((CH, D), F32),
        pltpu.VMEM((CH, D), BF16),
        pltpu.VMEM((32, D), BF16),
        pltpu.VMEM((HALF, CLIPS * THIRD), F32),
        pltpu.VMEM((8, 128), F32),
        pltpu.VMEM((CLIPS, 8, 128), F32),
        pltpu.VMEM((CH, TOK), BF16),
        pltpu.VMEM((TOK, CH), BF16),
        pltpu.VMEM((TOK, D), BF16),
        pltpu.VMEM((1, D), F32),
        pltpu.VMEM((8, 128), F32),
        pltpu.VMEM((TOK, H), F32),
        pltpu.VMEM((TOK, D), BF16),
        pltpu.VMEM((TOK, H), BF16),
        pltpu.VMEM((ROWS, SL), F32),
        pltpu.VMEM((CH, D), F32),
        dma((8,)), dma((7,)), dma((8,)), dma((NC,)), dma((NC,)), dma, dma,
        dma((9,)), dma((5,)), dma((16,)), dma((16,)), dma((16,)),
        dma((NZ,)), dma((NZ,)), dma((4,)), dma((4,)), dma((3,)), dma((3,)),
        dma((4 * NC,)), dma((4 * NC,)), dma((3 * NC,)), dma((3 * NC,)),
        dma((16,)), dma((16,)), dma((8,)), dma((8,)), dma, dma, dma((7,)), dma((8,)), dma((3,)), dma((4,)),
    ]
    return pl.pallas_call(
        kernel,
        name="fused_step",
        out_shape=(
            jax.ShapeDtypeStruct((TOK, D), BF16),
            jax.ShapeDtypeStruct((TOK, H), BF16),
            jax.ShapeDtypeStruct((ROWS, SL), F32),
            jax.ShapeDtypeStruct((CH, D), F32),
        ),
        in_specs=[sm, sm, vm, vm, vm, vm, vm, vm, anyspace, anyspace, anyspace],
        out_specs=(anyspace, anyspace, anyspace, anyspace),
        scratch_shapes=scratch,
        compiler_params=pltpu.CompilerParams(
            collective_id=0, has_side_effects=True, vmem_limit_bytes=58 * 2**20
        ),
    )(step, rewards, lat, noi, vc, vu, ew, gate, vals, w, cot)


def copy_kernel(bo, ga, gw, ge, bo_o, ga_o, gw_o, ge_o, v0, v1, v2, v3, ins, outs):
    loads, stores = [], []
    n = 0
    for src, mid, dst, parts in ((bo, v0, bo_o, 4), (ga, v1, ga_o, 2), (ge, v3, ge_o, 2), (gw, v2, gw_o, 1)):
        rows = src.shape[0] // parts
        for p in range(parts):
            at = pl.ds(p * rows, rows)
            loads.append(pltpu.make_async_copy(src.at[at], mid.at[at], ins.at[n]))
            stores.append(pltpu.make_async_copy(mid.at[at], dst.at[at], outs.at[n]))
            n += 1
    for c in loads:
        c.start()
    for a, b in zip(loads, stores):
        a.wait()
        b.start()
    for c in stores:
        c.wait()


def copied(*arrays):
    anyspace = pl.BlockSpec(memory_space=pl.ANY)
    return pl.pallas_call(
        copy_kernel,
        name="results",
        out_shape=tuple(jax.ShapeDtypeStruct(a.shape, a.dtype) for a in arrays),
        in_specs=[anyspace] * 4,
        out_specs=(anyspace,) * 4,
        scratch_shapes=[pltpu.VMEM(a.shape, a.dtype) for a in arrays]
        + [pltpu.SemaphoreType.DMA((9,)), pltpu.SemaphoreType.DMA((9,))],
        compiler_params=pltpu.CompilerParams(vmem_limit_bytes=60 * 2**20),
    )(*arrays)


def local(latent, sample_noise, vel_cond, vel_uncond, step_index, embed_w, gate_scale, attn_vals, out_w, cotangent, rewards):
    bo, ga, gw, ge = copied(*fused(
        step_index, rewards, latent[0], sample_noise[0], vel_cond[0], vel_uncond[0], embed_w,
        gate_scale, attn_vals[0], out_w, cotangent[0],
    ))
    return bo[None], ga[None], gw, ge[None]


def solution(mesh):
    in_specs = (
        P("clip", None, "seq"),
        P("clip", None, "seq"),
        P("clip", None, "seq"),
        P("clip", None, "seq"),
        P(),
        P(),
        P("clip", None),
        P("clip", "seq", None),
        P(None, "clip"),
        P("clip", "seq", None),
        P("clip"),
    )
    out_specs = (
        P("clip", "seq", None),
        P("clip", "seq", None),
        P("seq", "clip"),
        P("clip", None, None),
    )
    return jax.shard_map(local, mesh=mesh, in_specs=in_specs, out_specs=out_specs, check_vma=False)
```

time: 87.1 us -> 75.2 us (0.86)
  Pallas kernels: 79.8 us -> 73.2 us
  local copies, waits for them, and re-layouts: 5.15 us -> 0 us
    pallas_call x1, Pallas kernels: 79.8 us -> 70.3 us  [fused(): pl.pallas_call(kernel, name='fused_step', out_shape=(jax.ShapeDtypeStruct...]
    unnamed x10 -> x0, local copies, waits for them, and re-layouts: 5.15 us -> none
    pallas_call x0 -> x1, Pallas kernels: none -> 2.82 us  [copied(): pl.pallas_call(copy_kernel, name='results', out_shape=tuple((jax.ShapeDty...]
where the time goes in v2:
time: 75.2 us; the launch traced here: 75.1 us
  Pallas kernels  73.2 us (97%)
  between operations  1.93 us (3%)
    pallas_call x1, Pallas kernels, fused(): pl.pallas_call(kernel, name='fused_step', out_shape=(jax.ShapeDtypeStruct...  70.3 us
    pallas_call x1, Pallas kernels, copied(): pl.pallas_call(copy_kernel, name='results', out_shape=tuple((jax.ShapeDty...  2.82 us

profile of v2, /device:TPU:1, one launch (start us, length us, event | category | flops | bytes accessed | tf_op | source)
XLA Modules:
  0.0 75.1 jit_solution(9552381986970618185)
XLA Ops:
  1.9 70.3 %fused_step.1 = (bf16[256,3072]{1,0:T(8,128)(2,1)}, bf16[256,1536]{1,0:T(8,128)(2,1)}, f32[48,384]{1,0:T(8,128)}, f32[64,3072]{1,0:T(8,128)}) custom-call(s32[1]{0:T(128)S(6)} %copy.15.step_ref, f32[1]{0:T(128)S(6)} %copy.16.rew_ref, f32[64,256]{1,0:T(8,128)} %bitcast.11, f32[64,256]{1,0:T(8,128)} %bitcast.12, bf16[64,256]{1,0:T(8,128)(2,1)} %bitcast.13, ...), custom_call_target="tpu_custom_call" | custom-call | tf_op jit(solution)/shard_map/fused_step/pallas_call | solution.py:583
  72.3 2.8 %results.1 = (bf16[256,3072]{1,0:T(8,128)(2,1)}, bf16[256,1536]{1,0:T(8,128)(2,1)}, f32[48,384]{1,0:T(8,128)}, f32[64,3072]{1,0:T(8,128)}) custom-call(bf16[256,3072]{1,0:T(8,128)(2,1)} %get-tuple-element.12.bo, bf16[256,1536]{1,0:T(8,128)(2,1)} %get-tuple-element.13.ga, f32[48,384]{1,0:T(8,128)} %get-tuple-element.14.gw, f32[64,3072]{1,0:T(8,128)} %get-tuple-element.15.ge), custom_call_target="tpu_custom_call" | custom-call | tf_op jit(solution)/shard_map/results/pallas_call | solution.py:622

commit v3 on v2

--- a/solution.py
+++ b/solution.py
@@ -24,11 +24,23 @@
 CC = D // NC
 TILE = 256
 QR = H // 4
-NARROW = 2 * SL // 3
-THIRD = SL - NARROW
-ZW = 2 * NARROW
-SW = CLIPS * THIRD + 128
+THIRD = SL // 3
+ZW = 3 * THIRD
+SW = NC * ZW + 128
 MESH = pl.DeviceIdType.MESH
+
+
+def mwidth(j):
+    return 2 * THIRD if j % 2 else THIRD
+
+
+def swidth(j):
+    return SL - mwidth(j)
+
+
+def soffset(j):
+    return (j // 4) * 2 * ZW + (0, 2 * THIRD, 4 * THIRD, 3 * THIRD)[j % 4]
+
 F32, BF16 = jnp.float32, jnp.bfloat16
 
 
@@ -42,9 +54,9 @@
 
 
 def kernel(
-    step_ref, rew_ref, lat_ref, noi_ref, vc_ref, vu_ref, ew_ref, gate_ref, vals_ref, w_ref, cot_ref,
+    step_in, rew_in, lat_in, noi_in, vc_in, vu_in, ew_in, gate_in, vals_ref, w_ref, cot_ref,
     bo_out, ga_out, gw_out, ge_out,
-    vals_v, cot2, a2, vts, wf, gs, es, zls, zlr, zss, zsr, fs, fr, fss, frs, ef,
+    step_ref, rew_ref, lat_ref, noi_ref, vc_ref, vu_ref, ew_ref, gate_ref, vals_v, cot2, a2, vts, wf, gs, es, zls, zlr, zss, zsr, fs, fr, fss, frs, ef,
     sss, ssr, szls, szlr, szss, szsr,
     e_own, eo, er, gside, rsb, rrb, samp, samp_t, branch, gadv, advb, ga_acc, bo_ref, ga_ref, gw_ref, ge_ref,
     loc, r_s, r_r, cot_s, cot_r, a2_s, a2_r, wx_s, wy_s, wc_s, w_r, wc_r,
@@ -67,13 +79,6 @@
         return pltpu.make_async_remote_copy(
             src_ref=src, dst_ref=dst, send_sem=ss, recv_sem=rs, device_id=to, device_id_type=MESH
         )
-
-    ld_vals = pltpu.make_async_copy(vals_ref, vals_v, loc.at[0])
-    ld_cot = pltpu.make_async_copy(cot_ref, cot2.at[pl.ds(0, TOK)], loc.at[1])
-    ld_w = pltpu.make_async_copy(w_ref, wf.at[clip], loc.at[2])
-    ld_vals.start()
-    ld_cot.start()
-    ld_w.start()
 
     bar = pltpu.get_barrier_semaphore()
     me16 = clip * 2 + lo
@@ -89,6 +94,20 @@
     for p in partners:
         pl.semaphore_signal(bar, inc=1, device_id=p, device_id_type=MESH)
 
+    ld_vals = pltpu.make_async_copy(vals_ref, vals_v, loc.at[0])
+    ld_cot = pltpu.make_async_copy(cot_ref, cot2.at[pl.ds(0, TOK)], loc.at[1])
+    ld_w = pltpu.make_async_copy(w_ref, wf.at[clip], loc.at[2])
+    ld_vals.start()
+    ld_cot.start()
+    ld_w.start()
+    small = ((step_in, step_ref), (rew_in, rew_ref), (lat_in, lat_ref), (noi_in, noi_ref),
+             (vc_in, vc_ref), (vu_in, vu_ref), (ew_in, ew_ref), (gate_in, gate_ref))
+    ld_small = [pltpu.make_async_copy(a, b, loc.at[8 + i]) for i, (a, b) in enumerate(small)]
+    for cp in ld_small:
+        cp.start()
+
+    for cp in ld_small[:6]:
+        cp.wait()
     rsb[...] = jnp.full((8, 128), rew_ref[0], F32)
     rrb[clip] = jnp.full((8, 128), rew_ref[0], F32)
     idx = jnp.full((1, TOK), step_ref[0], jnp.int32)
@@ -223,7 +242,8 @@
         return rcopy(ef.at[me4], ef.at[me4], e4_s.at[i], e4_r.at[me4], to)
 
     def fs_copy(j):
-        return rcopy(fss.at[j], frs.at[clip], f2_s.at[j], f2_r.at[clip], (j, seq))
+        w = pl.ds(0, swidth(j))
+        return rcopy(fss.at[j, :, w], frs.at[clip, :, w], f2_s.at[j], f2_r.at[clip], (j, seq))
 
     def side_copy(i):
         return rcopy(sss.at[i], ssr.at[i], ss_s.at[i], ss_r.at[i], side)
@@ -262,13 +282,13 @@
         sshort(2).wait_recv()
         v = sown(z, lo) + ssr[7].astype(F32) + szlr[3].astype(F32) + szsr[2].astype(F32)
         for j in range(CLIPS):
-            o = j * SL + NARROW
-            fss[j] = (v[:, j * THIRD:(j + 1) * THIRD] * gadv[:, o:o + THIRD]).astype(BF16)
+            o, w, c = j * SL + mwidth(j), swidth(j), soffset(j)
+            fss[j, :, :w] = (v[:, c:c + w] * gadv[:, o:o + w]).astype(BF16)
 
             @pl.when(clip != j)
             def _():
                 fs_copy(j).start()
-        emb = v[:, CLIPS * THIRD:].astype(BF16)
+        emb = v[:, NC * ZW:].astype(BF16)
         ef[me4, z] = jnp.concatenate([emb[i * 16:(i + 1) * 16] for i in range(3)], axis=1)
         for r in range(1, NZ):
             e3_copy(r).start()
@@ -283,6 +303,7 @@
         adv = rrb[clip] - total / CLIPS
         advb[...] = adv
         adv1 = adv[0:1, 0:1]
+        ld_small[7].wait()
         gadv[...] = gate_ref[...] * adv1
 
     def e_first():
@@ -303,35 +324,42 @@
         e1_copy().wait_recv()
         es[...] = e_own[pl.ds(pl.multiple_of(core * 32, 32), 32), :] + er[...].astype(F32)
 
+    def dot_cols(*pieces):
+        parts = [cot2[:, a:a + w] for a, w in pieces]
+        rhs = parts[0] if len(parts) == 1 else jnp.concatenate(parts, axis=1)
+        return jnp.dot(a2[...], rhs, preferred_element_type=F32)
+
     def g_chunk(k):
-        def tile(j, carry):
-            cols = pl.ds(pl.multiple_of((2 * k + j) * SL, 128), NARROW)
-            g = jnp.dot(a2[...], cot2[:, cols], preferred_element_type=F32)
-            gs[k, :, pl.ds(pl.multiple_of(j * NARROW, NARROW), NARROW)] = g
-            return carry
-        lax.fori_loop(0, 2, tile, 0)
+        gs[k, :, :2 * THIRD] = dot_cols(((2 * k + 1) * SL, 2 * THIRD))
+        gs[k, :, 2 * THIRD:] = dot_cols((2 * k * SL, THIRD))
 
     def g_side():
-        def tile(j, carry):
-            parts = [cot2[:, pl.ds(pl.multiple_of((2 * j + i) * SL + NARROW, 128), THIRD)] for i in range(2)]
-            g = jnp.dot(a2[...], jnp.concatenate(parts, axis=1), preferred_element_type=F32)
-            gside[:, pl.ds(pl.multiple_of(j * 2 * THIRD, 2 * THIRD), 2 * THIRD)] = g
-            return carry
-        lax.fori_loop(0, NC, tile, 0)
+        for m in range(2):
+            o = m * 2 * ZW
+            j = 4 * m
+            gside[:, o:o + 2 * THIRD] = dot_cols((j * SL + THIRD, 2 * THIRD))
+            gside[:, o + 2 * THIRD:o + 4 * THIRD] = dot_cols(
+                ((j + 1) * SL + 2 * THIRD, THIRD), ((j + 3) * SL + 2 * THIRD, THIRD)
+            )
+            gside[:, o + 4 * THIRD:o + 6 * THIRD] = dot_cols(((j + 2) * SL + THIRD, 2 * THIRD))
 
     def f_copy(q):
         to = (q // 2, z * 4 + (q % 2) * 2 + core)
-        return rcopy(fs.at[q], fr.at[me16], f_s.at[q], f_r.at[me16], to)
+        w = pl.ds(0, mwidth(q // 2))
+        return rcopy(fs.at[q, :, w], fr.at[me16, :, w], f_s.at[q], f_r.at[me16], to)
 
     def final(k):
         zlong(3, k).wait_recv()
         zshort(2, k).wait_recv()
         both = gs[k, zrows(z), :] + zlr[3, k].astype(F32) + zsr[2, k].astype(F32)
         for j in range(2):
-            r = both[:, j * NARROW:(j + 1) * NARROW] * gadv[:, k * CC + j * SL:k * CC + j * SL + NARROW]
+            jj = 2 * k + j
+            w = mwidth(jj)
+            r = both[:, :w] if j else both[:, 2 * THIRD:]
+            r = r * gadv[:, jj * SL:jj * SL + w]
             for l in range(2):
                 q = (2 * k + j) * 2 + l
-                fs[q] = r[l * ROWS:(l + 1) * ROWS].astype(BF16)
+                fs[q, :, :w] = r[l * ROWS:(l + 1) * ROWS].astype(BF16)
 
                 @pl.when(me16 != q)
                 def _():
@@ -420,71 +448,76 @@
         g_chunk(k)
         zstep(0, k)
     zstep(1, 0)
+    advantage()
     stage_1()
-    advantage()
+    ld_small[6].wait()
     scaled = (cot2[pl.ds(0, TOK), :].astype(F32) * advb[0:1, 0:1]).astype(BF16)
     branch[...] = (scaled.astype(F32) * gate_ref[...]).astype(BF16)
+    zstep(1, 1)
     sstep(0)
-    zstep(1, 1)
+    stage_2b()
+    stage_2()
+    w_use(clip, first=True, own=True)
+    zstep(2, 0)
+    zstep(1, 3)
+    w_use(a_slot(3))
     zstep(1, 2)
-    stage_2()
-    stage_2b()
-    w_use(clip, first=True, own=True)
-    zstep(1, 3)
+    sstep(1)
+    w_use(b_slot(0))
+    zstep(3, 0)
+    w_use(a_slot(1))
     stage_3()
-    w_use(a_slot(1))
-    zstep(2, 0)
     stage_5(1)
-    w_use(a_slot(3))
-    sstep(1)
-    zstep(2, 1)
     stage_4()
-    w_use(b_slot(0))
-    zstep(2, 2)
-    w_use(a_slot(2))
-    zstep(2, 3)
-    zstep(3, 0)
     stage_5(3)
     stage_6()
+    zstep(2, 2)
+    zstep(2, 1)
+    sstep(2)
+    final(0)
     w_use(b_slot(1))
-    sstep(2)
+    zstep(2, 3)
+    w_use(a_slot(2))
+    stage_5(2)
+    sstep(3)
+    zstep(3, 2)
+    stage_8()
     zstep(3, 1)
-    stage_5(2)
-    stage_8()
     w_use(b_slot(3))
-    zstep(3, 2)
     zstep(3, 3)
+    sfinal()
+    final(2)
+    final(1)
+    final(3)
     w_use(b_slot(2))
     pltpu.make_async_copy(bo_ref, bo_out, loc.at[6]).start()
     ga_ref[...] = ga_acc[...].astype(BF16)
     pltpu.make_async_copy(ga_ref, ga_out, loc.at[7]).start()
-    final(0)
-    sstep(3)
-    final(1)
-    final(2)
-    final(3)
-    sfinal()
     e_four()
     e_five()
 
     fr[me16] = fs[me16]
     frs[clip] = fss[clip]
-    for q in range(16):
-        @pl.when(me16 != q)
+    for par in range(2):
+        @pl.when(lax.rem(clip, 2) == par)
         def _():
-            rcopy(fs.at[q], fr.at[q], f_s.at[q], f_r.at[q], core_dev).wait_recv()
-    for j in range(CLIPS):
-        @pl.when(clip != j)
-        def _():
-            rcopy(fss.at[j], frs.at[j], f2_s.at[j], f2_r.at[j], core_dev).wait_recv()
-    acc = fr[0].astype(F32)
-    for q in range(1, 16):
-        acc = acc + fr[q].astype(F32)
-    gw_ref[:, :NARROW] = acc
-    acc = frs[0].astype(F32)
-    for j in range(1, CLIPS):
-        acc = acc + frs[j].astype(F32)
-    gw_ref[:, NARROW:] = acc
+            wm, ws = pl.ds(0, mwidth(par)), pl.ds(0, swidth(par))
+            for q in range(16):
+                @pl.when(me16 != q)
+                def _():
+                    rcopy(fs.at[q, :, wm], fr.at[q, :, wm], f_s.at[q], f_r.at[q], core_dev).wait_recv()
+            for j in range(CLIPS):
+                @pl.when(clip != j)
+                def _():
+                    rcopy(fss.at[j, :, ws], frs.at[j, :, ws], f2_s.at[j], f2_r.at[j], core_dev).wait_recv()
+            acc = fr[0, :, wm].astype(F32)
+            for q in range(1, 16):
+                acc = acc + fr[q, :, wm].astype(F32)
+            gw_ref[:, :mwidth(par)] = acc
+            acc = frs[0, :, ws].astype(F32)
+            for j in range(1, CLIPS):
+                acc = acc + frs[j, :, ws].astype(F32)
+            gw_ref[:, mwidth(par):] = acc
     pltpu.make_async_copy(gw_ref, gw_out, loc.at[5]).start()
 
     pltpu.make_async_copy(ge_ref, ge_out, loc.at[4]).wait()
@@ -531,11 +564,17 @@
 
 
 def fused(step, rewards, lat, noi, vc, vu, ew, gate, vals, w, cot):
-    vm = pl.BlockSpec(memory_space=pltpu.VMEM)
-    sm = pl.BlockSpec(memory_space=pltpu.SMEM)
     anyspace = pl.BlockSpec(memory_space=pl.ANY)
     dma = pltpu.SemaphoreType.DMA
     scratch = [
+        pltpu.SMEM((1,), jnp.int32),
+        pltpu.SMEM((1,), F32),
+        pltpu.VMEM((CH, TOK), F32),
+        pltpu.VMEM((CH, TOK), F32),
+        pltpu.VMEM((CH, TOK), BF16),
+        pltpu.VMEM((CH, TOK), BF16),
+        pltpu.VMEM((CH, D), BF16),
+        pltpu.VMEM((1, D), F32),
         pltpu.VMEM((TOK, H), BF16),
         pltpu.VMEM((2 * TOK, D), BF16),
         pltpu.VMEM((HALF, 2 * TOK), BF16),
@@ -547,10 +586,10 @@
         pltpu.VMEM((4, NC, ZROWS, ZW), BF16),
         pltpu.VMEM((3, NC, ZROWS, ZW), BF16),
         pltpu.VMEM((3, NC, ZROWS, ZW), BF16),
-        pltpu.VMEM((16, ROWS, NARROW), BF16),
-        pltpu.VMEM((16, ROWS, NARROW), BF16),
-        pltpu.VMEM((CLIPS, ROWS, THIRD), BF16),
-        pltpu.VMEM((CLIPS, ROWS, THIRD), BF16),
+        pltpu.VMEM((16, ROWS, 2 * THIRD), BF16),
+        pltpu.VMEM((16, ROWS, 2 * THIRD), BF16),
+        pltpu.VMEM((CLIPS, ROWS, 2 * THIRD), BF16),
+        pltpu.VMEM((CLIPS, ROWS, 2 * THIRD), BF16),
         pltpu.VMEM((4, NZ, 16, SL), BF16),
         pltpu.VMEM((NZ, ROWS, SW), BF16),
         pltpu.VMEM((NZ, ROWS, SW), BF16),
@@ -561,7 +600,7 @@
         pltpu.VMEM((CH, D), F32),
         pltpu.VMEM((CH, D), BF16),
         pltpu.VMEM((32, D), BF16),
-        pltpu.VMEM((HALF, CLIPS * THIRD), F32),
+        pltpu.VMEM((HALF, NC * ZW), F32),
         pltpu.VMEM((8, 128), F32),
         pltpu.VMEM((CLIPS, 8, 128), F32),
         pltpu.VMEM((CH, TOK), BF16),
@@ -574,7 +613,7 @@
         pltpu.VMEM((TOK, H), BF16),
         pltpu.VMEM((ROWS, SL), F32),
         pltpu.VMEM((CH, D), F32),
-        dma((8,)), dma((7,)), dma((8,)), dma((NC,)), dma((NC,)), dma, dma,
+        dma((16,)), dma((7,)), dma((8,)), dma((NC,)), dma((NC,)), dma, dma,
         dma((9,)), dma((5,)), dma((16,)), dma((16,)), dma((16,)),
         dma((NZ,)), dma((NZ,)), dma((4,)), dma((4,)), dma((3,)), dma((3,)),
         dma((4 * NC,)), dma((4 * NC,)), dma((3 * NC,)), dma((3 * NC,)),
@@ -589,7 +628,7 @@
             jax.ShapeDtypeStruct((ROWS, SL), F32),
             jax.ShapeDtypeStruct((CH, D), F32),
         ),
-        in_specs=[sm, sm, vm, vm, vm, vm, vm, vm, anyspace, anyspace, anyspace],
+        in_specs=[anyspace] * 11,
         out_specs=(anyspace, anyspace, anyspace, anyspace),
         scratch_shapes=scratch,
         compiler_params=pltpu.CompilerParams(

time: 75.2 us -> 70.9 us (0.943)
  Pallas kernels: 73.2 us -> 68.2 us
    pallas_call x1, Pallas kernels: 70.3 us -> 65.4 us  [fused(): pl.pallas_call(kernel, name='fused_step', out_shape=(jax.ShapeDtypeStruct...]
where the time goes in v3:
time: 70.9 us; the launch traced here: 70.1 us
  Pallas kernels  68.2 us (96%)
  between operations  1.93 us (3%)
    pallas_call x1, Pallas kernels, fused(): pl.pallas_call(kernel, name='fused_step', out_shape=(jax.ShapeDtypeStruct...  65.4 us
    pallas_call x1, Pallas kernels, copied(): pl.pallas_call(copy_kernel, name='results', out_shape=tuple((jax.ShapeDty...  2.82 us

profile of v3, /device:TPU:1, one launch (start us, length us, event | category | flops | bytes accessed | tf_op | source)
XLA Modules:
  0.0 70.1 jit_solution(10343435562270508521)
XLA Ops:
  1.9 65.4 %fused_step.1 = (bf16[256,3072]{1,0:T(8,128)(2,1)}, bf16[256,1536]{1,0:T(8,128)(2,1)}, f32[48,384]{1,0:T(8,128)}, f32[64,3072]{1,0:T(8,128)}) custom-call(s32[1]{0:T(128)S(6)} %copy.15.step_in, f32[1]{0:T(128)S(6)} %copy.16.rew_in, f32[64,256]{1,0:T(8,128)} %bitcast.11, f32[64,256]{1,0:T(8,128)} %bitcast.12, bf16[64,256]{1,0:T(8,128)(2,1)} %bitcast.13, ...), custom_call_target="tpu_custom_call" | custom-call | tf_op jit(solution)/shard_map/fused_step/pallas_call | solution.py:622
  67.3 2.8 %results.1 = (bf16[256,3072]{1,0:T(8,128)(2,1)}, bf16[256,1536]{1,0:T(8,128)(2,1)}, f32[48,384]{1,0:T(8,128)}, f32[64,3072]{1,0:T(8,128)}) custom-call(bf16[256,3072]{1,0:T(8,128)(2,1)} %get-tuple-element.12.bo, bf16[256,1536]{1,0:T(8,128)(2,1)} %get-tuple-element.13.ga, f32[48,384]{1,0:T(8,128)} %get-tuple-element.14.gw, f32[64,3072]{1,0:T(8,128)} %get-tuple-element.15.ge), custom_call_target="tpu_custom_call" | custom-call | tf_op jit(solution)/shard_map/results/pallas_call | solution.py:661

commit v4 on v3

--- a/solution.py
+++ b/solution.py
@@ -26,7 +26,8 @@
 QR = H // 4
 THIRD = SL // 3
 ZW = 3 * THIRD
-SW = NC * ZW + 128
+SW = NC * ZW
+
 MESH = pl.DeviceIdType.MESH
 
 
@@ -56,11 +57,11 @@
 def kernel(
     step_in, rew_in, lat_in, noi_in, vc_in, vu_in, ew_in, gate_in, vals_ref, w_ref, cot_ref,
     bo_out, ga_out, gw_out, ge_out,
-    step_ref, rew_ref, lat_ref, noi_ref, vc_ref, vu_ref, ew_ref, gate_ref, vals_v, cot2, a2, vts, wf, gs, es, zls, zlr, zss, zsr, fs, fr, fss, frs, ef,
+    step_ref, rew_ref, lat_ref, noi_ref, vc_ref, vu_ref, ew_ref, gate_ref, vals_v, cot2, a2, vts, wf, gs, es, zls, zlr, zss, zsr, fs, fr, fss, frs, ef, ehs, ehr, e2s, e2r,
     sss, ssr, szls, szlr, szss, szsr,
     e_own, eo, er, gside, rsb, rrb, samp, samp_t, branch, gadv, advb, ga_acc, bo_ref, ga_ref, gw_ref, ge_ref,
     loc, r_s, r_r, cot_s, cot_r, a2_s, a2_r, wx_s, wy_s, wc_s, w_r, wc_r,
-    ss_s, ss_r, szl_s, szl_r, szs_s, szs_r, zl_s, zl_r, zs_s, zs_r, f_s, f_r, f2_s, f2_r, e1_s, e1_r, e3_s, e3_r, e4_s, e4_r,
+    ss_s, ss_r, szl_s, szl_r, szs_s, szs_r, zl_s, zl_r, zs_s, zs_r, f_s, f_r, f2_s, f2_r, bo_s, e1_s, e1_r, eh_s, eh_r, e2_s, e2_r, e3_s, e3_r, e4_s, e4_r,
 ):
     clip = lax.axis_index("clip")
     seq = lax.axis_index("seq")
@@ -224,11 +225,7 @@
         return pl.ds(pl.multiple_of(d * ZROWS + l * ROWS, ROWS), ROWS)
 
     def sown(d, l):
-        emb = []
-        for i in range(3):
-            cols = pl.ds(pl.multiple_of(d * SL + i * 128, 128), 128)
-            emb.append(es[pl.ds(pl.multiple_of(l * 16, 16), 16), cols])
-        return jnp.concatenate([gside[lrows(d, l), :], jnp.concatenate(emb, axis=0)], axis=1)
+        return gside[lrows(d, l), :]
 
     sorder = (sgn * 4, -sgn * 3, sgn * 3, -sgn * 2, sgn * 2, -sgn, sgn, 0)
 
@@ -248,9 +245,9 @@
     def side_copy(i):
         return rcopy(sss.at[i], ssr.at[i], ss_s.at[i], ss_r.at[i], side)
 
-    def side_send():
-        for i, n in enumerate(sorder):
-            sss[i] = sown(zr(n), olo).astype(BF16)
+    def side_send(first, end):
+        for i in range(first, end):
+            sss[i] = sown(zr(sorder[i]), olo).astype(BF16)
             side_copy(i).start()
 
     def slong(t):
@@ -259,7 +256,7 @@
     def sshort(t):
         return rcopy(szss.at[t], szsr.at[t], szs_s.at[t], szs_r.at[t], zs_dev)
 
-    def sstep(t):
+    def splong(t):
         side_copy(2 * t).wait_recv()
         v = sown(zr(sgn * (4 - t)), lo) + ssr[2 * t].astype(F32)
         if t:
@@ -267,14 +264,15 @@
             v = v + szlr[t - 1].astype(F32)
         szls[t] = v.astype(BF16)
         slong(t).start()
-        if t < 3:
-            side_copy(2 * t + 1).wait_recv()
-            v = sown(zr(-sgn * (3 - t)), lo) + ssr[2 * t + 1].astype(F32)
-            if t:
-                sshort(t - 1).wait_recv()
-                v = v + szsr[t - 1].astype(F32)
-            szss[t] = v.astype(BF16)
-            sshort(t).start()
+
+    def spshort(t):
+        side_copy(2 * t + 1).wait_recv()
+        v = sown(zr(-sgn * (3 - t)), lo) + ssr[2 * t + 1].astype(F32)
+        if t:
+            sshort(t - 1).wait_recv()
+            v = v + szsr[t - 1].astype(F32)
+        szss[t] = v.astype(BF16)
+        sshort(t).start()
 
     def sfinal():
         side_copy(7).wait_recv()
@@ -288,8 +286,30 @@
             @pl.when(clip != j)
             def _():
                 fs_copy(j).start()
-        emb = v[:, NC * ZW:].astype(BF16)
-        ef[me4, z] = jnp.concatenate([emb[i * 16:(i + 1) * 16] for i in range(3)], axis=1)
+
+    def eh_copy():
+        return rcopy(ehs, ehr, eh_s, eh_r, side)
+
+    def e2_copy(r):
+        return rcopy(e2s.at[zr(r)], e2r.at[z], e2_s.at[r - 1], e2_r.at[z], dev(x, h, lo, zr(r), core))
+
+    def e_two():
+        eh_copy().wait_recv()
+        part = es[pl.ds(pl.multiple_of(lo * 16, 16), 16), :] + ehr[...].astype(F32)
+        for d in range(NZ):
+            e2s[d] = part[:, d * SL:(d + 1) * SL].astype(BF16)
+        for r in range(1, NZ):
+            e2_copy(r).start()
+        e2r[z] = e2s[z]
+
+    def e_three():
+        for r in range(1, NZ):
+            o = zr(r)
+            rcopy(e2s.at[o], e2r.at[o], e2_s.at[r - 1], e2_r.at[o], dev(x, h, lo, o, core)).wait_recv()
+        tot = e2r[0].astype(F32)
+        for d in range(1, NZ):
+            tot = tot + e2r[d].astype(F32)
+        ef[me4, z] = tot.astype(BF16)
         for r in range(1, NZ):
             e3_copy(r).start()
 
@@ -323,6 +343,8 @@
     def e_sum():
         e1_copy().wait_recv()
         es[...] = e_own[pl.ds(pl.multiple_of(core * 32, 32), 32), :] + er[...].astype(F32)
+        ehs[...] = es[pl.ds(pl.multiple_of(olo * 16, 16), 16), :].astype(BF16)
+        eh_copy().start()
 
     def dot_cols(*pieces):
         parts = [cot2[:, a:a + w] for a, w in pieces]
@@ -365,7 +387,11 @@
                 def _():
                     f_copy(q).start()
 
-    def w_use(slot, first=False, own=False):
+    def bo_copy(slot):
+        cols = pl.ds(pl.multiple_of(slot * SL, SL), SL)
+        return pltpu.make_async_copy(bo_ref.at[:, cols], bo_out.at[:, cols], bo_s.at[slot])
+
+    def w_use(slot, first=False, own=False, last=False):
         if own:
             ld_w.wait()
         else:
@@ -376,12 +402,16 @@
         emb = jnp.dot(samp_t[...], ew_ref[:, cols], preferred_element_type=F32)
         bo_ref[:, cols] = (emb + gate_ref[:, cols] * proj).astype(BF16)
         br = branch[:, cols]
+        bo_copy(slot).start()
         for i in range(2):
-            g = lax.dot_general(br, wf[slot, i * HALF:(i + 1) * HALF], (((1,), (1,)), ((), ())), preferred_element_type=F32)
+            half = slice(i * HALF, (i + 1) * HALF)
+            g = lax.dot_general(br, wf[slot, half], (((1,), (1,)), ((), ())), preferred_element_type=F32)
             if first:
-                ga_acc[:, i * HALF:(i + 1) * HALF] = g
+                ga_acc[:, half] = g
+            elif last:
+                ga_ref[:, half] = (ga_acc[:, half] + g).astype(BF16)
             else:
-                ga_acc[:, i * HALF:(i + 1) * HALF] += g
+                ga_acc[:, half] += g
 
     def e_four():
         for r in range(1, NZ):
@@ -439,61 +469,69 @@
     cp_cot[0].wait_recv()
     g_chunk(0)
     zstep(0, 0)
-    for k in range(1, NC):
-        cp_cot[k].wait_recv()
+    cp_cot[2].wait_recv()
+    g_chunk(2)
+    zstep(0, 2)
+    cp_cot[1].wait_recv()
+    cp_cot[3].wait_recv()
     g_side()
+    side_send(0, 2)
     e_sum()
-    side_send()
-    for k in range(1, NC):
-        g_chunk(k)
-        zstep(0, k)
+    side_send(2, 8)
+    g_chunk(1)
+    zstep(0, 1)
+    g_chunk(3)
+    zstep(0, 3)
+    stage_1()
+    zstep(1, 2)
+    advantage()
     zstep(1, 0)
-    advantage()
-    stage_1()
     ld_small[6].wait()
     scaled = (cot2[pl.ds(0, TOK), :].astype(F32) * advb[0:1, 0:1]).astype(BF16)
     branch[...] = (scaled.astype(F32) * gate_ref[...]).astype(BF16)
+    splong(0)
+    zstep(1, 3)
     zstep(1, 1)
-    sstep(0)
     stage_2b()
+    e_two()
+    zstep(2, 2)
+    spshort(0)
     stage_2()
-    w_use(clip, first=True, own=True)
     zstep(2, 0)
-    zstep(1, 3)
+    w_use(b_slot(0), first=True)
+    splong(1)
+    zstep(2, 3)
+    stage_3()
+    w_use(clip, own=True)
+    zstep(2, 1)
+    w_use(a_slot(1))
+    stage_6()
+    e_three()
+    stage_5(1)
+    spshort(1)
+    zstep(3, 2)
+    stage_5(3)
     w_use(a_slot(3))
-    zstep(1, 2)
-    sstep(1)
-    w_use(b_slot(0))
+    splong(2)
+    stage_4()
     zstep(3, 0)
-    w_use(a_slot(1))
-    stage_3()
-    stage_5(1)
-    stage_4()
-    stage_5(3)
-    stage_6()
-    zstep(2, 2)
-    zstep(2, 1)
-    sstep(2)
+    zstep(3, 3)
+    w_use(b_slot(1))
+    zstep(3, 1)
+    stage_8()
+    spshort(2)
+    stage_5(2)
+    splong(3)
+    e_four()
+    final(2)
+    final(3)
     final(0)
-    w_use(b_slot(1))
-    zstep(2, 3)
-    w_use(a_slot(2))
-    stage_5(2)
-    sstep(3)
-    zstep(3, 2)
-    stage_8()
-    zstep(3, 1)
+    final(1)
     w_use(b_slot(3))
-    zstep(3, 3)
     sfinal()
-    final(2)
-    final(1)
-    final(3)
     w_use(b_slot(2))
-    pltpu.make_async_copy(bo_ref, bo_out, loc.at[6]).start()
-    ga_ref[...] = ga_acc[...].astype(BF16)
+    w_use(a_slot(2), last=True)
     pltpu.make_async_copy(ga_ref, ga_out, loc.at[7]).start()
-    e_four()
     e_five()
 
     fr[me16] = fs[me16]
@@ -522,7 +560,8 @@
 
     pltpu.make_async_copy(ge_ref, ge_out, loc.at[4]).wait()
     pltpu.make_async_copy(gw_ref, gw_out, loc.at[5]).wait()
-    pltpu.make_async_copy(bo_ref, bo_out, loc.at[6]).wait()
+    for j in range(CLIPS):
+        bo_copy(j).wait()
     pltpu.make_async_copy(ga_ref, ga_out, loc.at[7]).wait()
     for cp in rsends:
         cp.wait_send()
@@ -557,7 +596,9 @@
         def _():
             fs_copy(j).wait_send()
     e1_copy().wait_send()
+    eh_copy().wait_send()
     for r in range(1, NZ):
+        e2_copy(r).wait_send()
         e3_copy(r).wait_send()
     for i in range(3):
         e4_copy(i).wait_send()
@@ -591,6 +632,10 @@
         pltpu.VMEM((CLIPS, ROWS, 2 * THIRD), BF16),
         pltpu.VMEM((CLIPS, ROWS, 2 * THIRD), BF16),
         pltpu.VMEM((4, NZ, 16, SL), BF16),
+        pltpu.VMEM((16, D), BF16),
+        pltpu.VMEM((16, D), BF16),
+        pltpu.VMEM((NZ, 16, SL), BF16),
+        pltpu.VMEM((NZ, 16, SL), BF16),
         pltpu.VMEM((NZ, ROWS, SW), BF16),
         pltpu.VMEM((NZ, ROWS, SW), BF16),
         pltpu.VMEM((4, ROWS, SW), BF16),
@@ -617,7 +662,7 @@
         dma((9,)), dma((5,)), dma((16,)), dma((16,)), dma((16,)),
         dma((NZ,)), dma((NZ,)), dma((4,)), dma((4,)), dma((3,)), dma((3,)),
         dma((4 * NC,)), dma((4 * NC,)), dma((3 * NC,)), dma((3 * NC,)),
-        dma((16,)), dma((16,)), dma((8,)), dma((8,)), dma, dma, dma((7,)), dma((8,)), dma((3,)), dma((4,)),
+        dma((16,)), dma((16,)), dma((8,)), dma((8,)), dma((8,)), dma, dma, dma, dma, dma((7,)), dma((8,)), dma((7,)), dma((8,)), dma((3,)), dma((4,)),
     ]
     return pl.pallas_call(
         kernel,

time: 70.9 us -> 66.6 us (0.939)
  Pallas kernels: 68.2 us -> 64.3 us
    pallas_call x1, Pallas kernels: 65.4 us -> 61.5 us  [fused(): pl.pallas_call(kernel, name='fused_step', out_shape=(jax.ShapeDtypeStruct...]
where the time goes in v4:
time: 66.6 us; the launch traced here: 66.2 us
  Pallas kernels  64.3 us (97%)
  between operations  1.93 us (3%)
    pallas_call x1, Pallas kernels, fused(): pl.pallas_call(kernel, name='fused_step', out_shape=(jax.ShapeDtypeStruct...  61.5 us
    pallas_call x1, Pallas kernels, copied(): pl.pallas_call(copy_kernel, name='results', out_shape=tuple((jax.ShapeDty...  2.82 us

profile of v4, /device:TPU:1, one launch (start us, length us, event | category | flops | bytes accessed | tf_op | source)
XLA Modules:
  0.0 66.2 jit_solution(8811108045336779932)
XLA Ops:
  1.9 61.5 %fused_step.1 = (bf16[256,3072]{1,0:T(8,128)(2,1)}, bf16[256,1536]{1,0:T(8,128)(2,1)}, f32[48,384]{1,0:T(8,128)}, f32[64,3072]{1,0:T(8,128)}) custom-call(s32[1]{0:T(128)S(6)} %copy.15.step_in, f32[1]{0:T(128)S(6)} %copy.16.rew_in, f32[64,256]{1,0:T(8,128)} %bitcast.11, f32[64,256]{1,0:T(8,128)} %bitcast.12, bf16[64,256]{1,0:T(8,128)(2,1)} %bitcast.13, ...), custom_call_target="tpu_custom_call" | custom-call | tf_op jit(solution)/shard_map/fused_step/pallas_call | solution.py:667
  63.4 2.8 %results.1 = (bf16[256,3072]{1,0:T(8,128)(2,1)}, bf16[256,1536]{1,0:T(8,128)(2,1)}, f32[48,384]{1,0:T(8,128)}, f32[64,3072]{1,0:T(8,128)}) custom-call(bf16[256,3072]{1,0:T(8,128)(2,1)} %get-tuple-element.12.bo, bf16[256,1536]{1,0:T(8,128)(2,1)} %get-tuple-element.13.ga, f32[48,384]{1,0:T(8,128)} %get-tuple-element.14.gw, f32[64,3072]{1,0:T(8,128)} %get-tuple-element.15.ge), custom_call_target="tpu_custom_call" | custom-call | tf_op jit(solution)/shard_map/results/pallas_call | solution.py:706

commit v5 on v4

--- a/solution.py
+++ b/solution.py
@@ -534,35 +534,6 @@
     pltpu.make_async_copy(ga_ref, ga_out, loc.at[7]).start()
     e_five()
 
-    fr[me16] = fs[me16]
-    frs[clip] = fss[clip]
-    for par in range(2):
-        @pl.when(lax.rem(clip, 2) == par)
-        def _():
-            wm, ws = pl.ds(0, mwidth(par)), pl.ds(0, swidth(par))
-            for q in range(16):
-                @pl.when(me16 != q)
-                def _():
-                    rcopy(fs.at[q, :, wm], fr.at[q, :, wm], f_s.at[q], f_r.at[q], core_dev).wait_recv()
-            for j in range(CLIPS):
-                @pl.when(clip != j)
-                def _():
-                    rcopy(fss.at[j, :, ws], frs.at[j, :, ws], f2_s.at[j], f2_r.at[j], core_dev).wait_recv()
-            acc = fr[0, :, wm].astype(F32)
-            for q in range(1, 16):
-                acc = acc + fr[q, :, wm].astype(F32)
-            gw_ref[:, :mwidth(par)] = acc
-            acc = frs[0, :, ws].astype(F32)
-            for j in range(1, CLIPS):
-                acc = acc + frs[j, :, ws].astype(F32)
-            gw_ref[:, mwidth(par):] = acc
-    pltpu.make_async_copy(gw_ref, gw_out, loc.at[5]).start()
-
-    pltpu.make_async_copy(ge_ref, ge_out, loc.at[4]).wait()
-    pltpu.make_async_copy(gw_ref, gw_out, loc.at[5]).wait()
-    for j in range(CLIPS):
-        bo_copy(j).wait()
-    pltpu.make_async_copy(ga_ref, ga_out, loc.at[7]).wait()
     for cp in rsends:
         cp.wait_send()
     for cp in cp_cot:
@@ -602,6 +573,36 @@
         e3_copy(r).wait_send()
     for i in range(3):
         e4_copy(i).wait_send()
+
+    fr[me16] = fs[me16]
+    frs[clip] = fss[clip]
+    for par in range(2):
+        @pl.when(lax.rem(clip, 2) == par)
+        def _():
+            wm, ws = pl.ds(0, mwidth(par)), pl.ds(0, swidth(par))
+            for q in range(16):
+                @pl.when(me16 != q)
+                def _():
+                    rcopy(fs.at[q, :, wm], fr.at[q, :, wm], f_s.at[q], f_r.at[q], core_dev).wait_recv()
+            for j in range(CLIPS):
+                @pl.when(clip != j)
+                def _():
+                    rcopy(fss.at[j, :, ws], frs.at[j, :, ws], f2_s.at[j], f2_r.at[j], core_dev).wait_recv()
+            acc = fr[0, :, wm].astype(F32)
+            for q in range(1, 16):
+                acc = acc + fr[q, :, wm].astype(F32)
+            gw_ref[:, :mwidth(par)] = acc
+            acc = frs[0, :, ws].astype(F32)
+            for j in range(1, CLIPS):
+                acc = acc + frs[j, :, ws].astype(F32)
+            gw_ref[:, mwidth(par):] = acc
+    pltpu.make_async_copy(gw_ref, gw_out, loc.at[5]).start()
+
+    pltpu.make_async_copy(ge_ref, ge_out, loc.at[4]).wait()
+    pltpu.make_async_copy(gw_ref, gw_out, loc.at[5]).wait()
+    for j in range(CLIPS):
+        bo_copy(j).wait()
+    pltpu.make_async_copy(ga_ref, ga_out, loc.at[7]).wait()
 
 
 def fused(step, rewards, lat, noi, vc, vu, ew, gate, vals, w, cot):

time: 66.6 us -> 66.4 us (level)
  no operation moved by 1% of the time
where the time goes in v5:
time: 66.4 us; the launch traced here: 66 us
  Pallas kernels  64.1 us (97%)
  between operations  1.93 us (3%)
    pallas_call x1, Pallas kernels, fused(): pl.pallas_call(kernel, name='fused_step', out_shape=(jax.ShapeDtypeStruct...  61.3 us
    pallas_call x1, Pallas kernels, copied(): pl.pallas_call(copy_kernel, name='results', out_shape=tuple((jax.ShapeDty...  2.82 us

profile of v5, /device:TPU:1, one launch (start us, length us, event | category | flops | bytes accessed | tf_op | source)
XLA Modules:
  0.0 66.0 jit_solution(2346924423752721336)
XLA Ops:
  1.9 61.3 %fused_step.1 = (bf16[256,3072]{1,0:T(8,128)(2,1)}, bf16[256,1536]{1,0:T(8,128)(2,1)}, f32[48,384]{1,0:T(8,128)}, f32[64,3072]{1,0:T(8,128)}) custom-call(s32[1]{0:T(128)S(6)} %copy.15.step_in, f32[1]{0:T(128)S(6)} %copy.16.rew_in, f32[64,256]{1,0:T(8,128)} %bitcast.11, f32[64,256]{1,0:T(8,128)} %bitcast.12, bf16[64,256]{1,0:T(8,128)(2,1)} %bitcast.13, ...), custom_call_target="tpu_custom_call" | custom-call | tf_op jit(solution)/shard_map/fused_step/pallas_call | solution.py:668
  63.2 2.8 %results.1 = (bf16[256,3072]{1,0:T(8,128)(2,1)}, bf16[256,1536]{1,0:T(8,128)(2,1)}, f32[48,384]{1,0:T(8,128)}, f32[64,3072]{1,0:T(8,128)}) custom-call(bf16[256,3072]{1,0:T(8,128)(2,1)} %get-tuple-element.12.bo, bf16[256,1536]{1,0:T(8,128)(2,1)} %get-tuple-element.13.ga, f32[48,384]{1,0:T(8,128)} %get-tuple-element.14.gw, f32[64,3072]{1,0:T(8,128)} %get-tuple-element.15.ge), custom_call_target="tpu_custom_call" | custom-call | tf_op jit(solution)/shard_map/results/pallas_call | solution.py:707

commit v6 on v5

--- a/solution.py
+++ b/solution.py
@@ -584,14 +584,14 @@
                 @pl.when(me16 != q)
                 def _():
                     rcopy(fs.at[q, :, wm], fr.at[q, :, wm], f_s.at[q], f_r.at[q], core_dev).wait_recv()
+            acc = fr[0, :, wm].astype(F32)
+            for q in range(1, 16):
+                acc = acc + fr[q, :, wm].astype(F32)
+            gw_ref[:, :mwidth(par)] = acc
             for j in range(CLIPS):
                 @pl.when(clip != j)
                 def _():
                     rcopy(fss.at[j, :, ws], frs.at[j, :, ws], f2_s.at[j], f2_r.at[j], core_dev).wait_recv()
-            acc = fr[0, :, wm].astype(F32)
-            for q in range(1, 16):
-                acc = acc + fr[q, :, wm].astype(F32)
-            gw_ref[:, :mwidth(par)] = acc
             acc = frs[0, :, ws].astype(F32)
             for j in range(1, CLIPS):
                 acc = acc + frs[j, :, ws].astype(F32)

time: 66.4 us -> 66.4 us (level)
  no operation moved by 1% of the time
where the time goes in v6:
time: 66.4 us; the launch traced here: 66 us
  Pallas kernels  64.1 us (97%)
  between operations  1.93 us (3%)
    pallas_call x1, Pallas kernels, fused(): pl.pallas_call(kernel, name='fused_step', out_shape=(jax.ShapeDtypeStruct...  61.2 us
    pallas_call x1, Pallas kernels, copied(): pl.pallas_call(copy_kernel, name='results', out_shape=tuple((jax.ShapeDty...  2.82 us

profile of v6, /device:TPU:1, one launch (start us, length us, event | category | flops | bytes accessed | tf_op | source)
XLA Modules:
  0.0 66.0 jit_solution(5665189013352374951)
XLA Ops:
  1.9 61.2 %fused_step.1 = (bf16[256,3072]{1,0:T(8,128)(2,1)}, bf16[256,1536]{1,0:T(8,128)(2,1)}, f32[48,384]{1,0:T(8,128)}, f32[64,3072]{1,0:T(8,128)}) custom-call(s32[1]{0:T(128)S(6)} %copy.15.step_in, f32[1]{0:T(128)S(6)} %copy.16.rew_in, f32[64,256]{1,0:T(8,128)} %bitcast.11, f32[64,256]{1,0:T(8,128)} %bitcast.12, bf16[64,256]{1,0:T(8,128)(2,1)} %bitcast.13, ...), custom_call_target="tpu_custom_call" | custom-call | tf_op jit(solution)/shard_map/fused_step/pallas_call | solution.py:668
  63.2 2.8 %results.1 = (bf16[256,3072]{1,0:T(8,128)(2,1)}, bf16[256,1536]{1,0:T(8,128)(2,1)}, f32[48,384]{1,0:T(8,128)}, f32[64,3072]{1,0:T(8,128)}) custom-call(bf16[256,3072]{1,0:T(8,128)(2,1)} %get-tuple-element.12.bo, bf16[256,1536]{1,0:T(8,128)(2,1)} %get-tuple-element.13.ga, f32[48,384]{1,0:T(8,128)} %get-tuple-element.14.gw, f32[64,3072]{1,0:T(8,128)} %get-tuple-element.15.ge), custom_call_target="tpu_custom_call" | custom-call | tf_op jit(solution)/shard_map/results/pallas_call | solution.py:707
